TPU v7x, 256 devices: a whole 4x4x8 slice. The times are simulated.
256 devices in a mesh: grid: 64 (over y, z, core), layer: 4 (over x).
Axes of the slice: x: 4, y: 4, z: 8, core: 2. Of those that a mesh axis runs over, the one named last changes fastest.
Arguments:
- h_vals: bfloat16 [256, 28, 128, 128], P('grid', 'layer'), may hold values from -0.09375 to 0.09375
- h_cols: int32 [256, 28], P('grid', 'layer'), may hold values from 0 to 255, as said below
- t_now: bfloat16 [256, 28, 128, 128], P(('grid', 'layer')), may hold values from -6 to 6
- t_prev: bfloat16 [256, 28, 128, 128], P(('grid', 'layer')), may hold values from -6 to 6
- t_cols: int32 [256, 28], replicated, may hold values from 0 to 255, as said below
- density: float32 [256, 28, 128, 128], P(('grid', 'layer')), may hold values from -6 to 6
- coefficient: float32 [1], replicated, may hold values from 0.5 to 1.5
Outputs:
- t_next: bfloat16 [256, 28, 128, 128], P(('grid', 'layer'))
- density_next: float32 [256, 28, 128, 128], P(('grid', 'layer'))
Inputs may be any that keep to these rules, and one draw needn't show every extreme that they name: Each row of h_cols holds distinct block columns within 15 of the row's own index, taken cyclically modulo 256; slots 7 l to 7 l + 6 hold columns c with c % 4 == l. Each row of t_cols holds distinct block columns within 15 of the row's own index, taken cyclically modulo 256.
All inputs are finite; a program needn't handle non-finite values.
Results may differ from a plain program's by a relative error of at most 0.0065.
Values may be sent and summed in bfloat16 or wider, within the bound.
No kernel may reach another device: no remote copies, remote signals or barrier semaphores. Data moves between devices by JAX's collectives and lax.ppermute only.
A program may use at most 128 MiB of HBM per device.

v0:
```python
import jax
import jax.numpy as jnp
from jax import lax
from jax.sharding import PartitionSpec as P

HW = 15


def passed_along(block, axis, distance):
    devices = range(lax.axis_size(axis))
    route = [((i - distance) % len(devices), i) for i in devices]
    return lax.ppermute(block, axis, route)


def shards(h_vals, h_cols, t_now, t_prev, t_cols, density, coefficient):
    own_rows = t_now.shape[0]
    stored = t_now.shape[1]
    block = t_now.shape[2]
    layers = lax.axis_size("layer")
    grid_size = lax.axis_size("grid")
    group_rows = own_rows * layers
    reach = (HW + group_rows - 1) // group_rows
    grid_pos = lax.axis_index("grid")
    pieces = []
    for offset in range(-reach, reach + 1):
        if offset == 0:
            pieces.append(t_now)
        else:
            pieces.append(passed_along(t_now, "grid", -offset))
    stacked = jnp.stack(pieces).reshape((2 * reach + 1) * own_rows * stored, block, block)
    slots = jnp.arange(stored, dtype=jnp.int32)

    def row_term(local_row):
        cols = lax.dynamic_index_in_dim(h_cols, local_row, 0, keepdims=False)
        values = lax.dynamic_index_in_dim(h_vals, local_row, 0, keepdims=False)
        wanted = t_cols[grid_pos * group_rows + local_row]
        present = t_cols[cols]
        equal = wanted[None, :, None] == present[:, None, :]
        pick = jnp.sum(jnp.where(equal, slots[None, None, :], 0), axis=2)
        valid = jnp.any(equal, axis=2)
        distance = (cols // group_rows - grid_pos) % grid_size
        distance = jnp.where(distance > grid_size // 2, distance - grid_size, distance)
        source = (distance + reach) * own_rows + cols % own_rows
        index = source[:, None] * stored + pick
        chosen = jnp.where(valid[:, :, None, None], stacked[index], jnp.zeros((), stacked.dtype))
        return jnp.einsum("hab,hsbc->sac", values, chosen, preferred_element_type=jnp.float32)

    partial_rows = lax.map(row_term, jnp.arange(group_rows, dtype=jnp.int32))
    summed = lax.psum_scatter(partial_rows, "layer", scatter_dimension=0, tiled=True)
    t_next = (2.0 * summed - t_prev.astype(jnp.float32)).astype(jnp.bfloat16)
    density_next = density + coefficient[0] * t_next.astype(jnp.float32)
    return (t_next, density_next)


def solution(mesh):
    placed = (
        P("grid", "layer", None, None),
        P("grid", "layer"),
        P(("grid", "layer"), None, None, None),
        P(("grid", "layer"), None, None, None),
        P(),
        P(("grid", "layer"), None, None, None),
        P(),
    )
    return jax.shard_map(
        shards,
        mesh=mesh,
        in_specs=placed,
        out_specs=(P(("grid", "layer"), None, None, None), P(("grid", "layer"), None, None, None)),
        check_vma=False,
    )
```

profile of v0, /device:TPU:1, one launch (start us, length us, event | category | flops | bytes accessed | tf_op | source)
XLA Modules:
  0.0 385.4 jit_solution(4909659814034772072)
XLA Ops:
  7.2 3.9 %collective-permute-start = (bf16[1,28,128,128]{3,2,1,0:T(8,128)(2,1)}, bf16[1,28,128,128]{3,2,1,0:T(8,128)(2,1)}, u32[]{:S(2)}, u32[]{:S(2)}) collective-permute-start(bf16[1,28,128,128]{3,2,1,0:T(8,128)(2,1)} %param.11), channel_id=1, source_target_pairs={{240,0},{244,4},{248,8},{252,12},{0,16},{4,20},{8,24},{12,28},{16,... | collective-permute-start | bytes 2752520 | tf_op jit(solution)/shard_map/ppermute | solution.py:12
  11.1 5.0 %collective-permute-start.1 = (bf16[1,28,128,128]{3,2,1,0:T(8,128)(2,1)}, bf16[1,28,128,128]{3,2,1,0:T(8,128)(2,1)}, u32[]{:S(2)}, u32[]{:S(2)}) collective-permute-start(bf16[1,28,128,128]{3,2,1,0:T(8,128)(2,1)} %param.11), channel_id=1, source_target_pairs={{244,0},{248,4},{252,8},{0,12},{4,16},{8,20},{12,24},{16,28},{20,3... | collective-permute-start | bytes 2752520 | tf_op jit(solution)/shard_map/ppermute | solution.py:12
  18.3 26.0 %collective-permute-done = bf16[1,28,128,128]{3,2,1,0:T(8,128)(2,1)} collective-permute-done((bf16[1,28,128,128]{3,2,1,0:T(8,128)(2,1)}, bf16[1,28,128,128]{3,2,1,0:T(8,128)(2,1)}, u32[]{:S(2)}, u32[]{:S(2)}) %collective-permute-start) | collective-permute-done | bytes 917536 | tf_op jit(solution)/shard_map/ppermute | solution.py:12
  44.3 16.2 %collective-permute-start.5 = (bf16[1,28,128,128]{3,2,1,0:T(8,128)(2,1)}, bf16[1,28,128,128]{3,2,1,0:T(8,128)(2,1)S(1)}, u32[]{:S(2)}, u32[]{:S(2)}) collective-permute-start(bf16[1,28,128,128]{3,2,1,0:T(8,128)(2,1)} %param.11), channel_id=1, source_target_pairs={{8,0},{12,4},{16,8},{20,12},{24,16},{28,20},{32,24},{36,28},{40,32... | collective-permute-start | bytes 2752520 | tf_op jit(solution)/shard_map/ppermute | solution.py:12
  61.8 25.0 %collective-permute-done.1 = bf16[1,28,128,128]{3,2,1,0:T(8,128)(2,1)} collective-permute-done((bf16[1,28,128,128]{3,2,1,0:T(8,128)(2,1)}, bf16[1,28,128,128]{3,2,1,0:T(8,128)(2,1)}, u32[]{:S(2)}, u32[]{:S(2)}) %collective-permute-start.1) | collective-permute-done | bytes 917536 | tf_op jit(solution)/shard_map/ppermute | solution.py:12
  86.8 1.8 collective-permute-start.6
  90.0 15.7 %collective-permute-done.2 = bf16[1,28,128,128]{3,2,1,0:T(8,128)(2,1)} collective-permute-done((bf16[1,28,128,128]{3,2,1,0:T(8,128)(2,1)}, bf16[1,28,128,128]{3,2,1,0:T(8,128)(2,1)}, u32[]{:S(2)}, u32[]{:S(2)}) %collective-permute-start.2) | collective-permute-done | bytes 917536 | tf_op jit(solution)/shard_map/ppermute | solution.py:12
  105.7 2.3 collective-permute-start.7
  110.9 27.6 %collective-permute-done.6 = bf16[1,28,128,128]{3,2,1,0:T(8,128)(2,1)S(1)} collective-permute-done((bf16[1,28,128,128]{3,2,1,0:T(8,128)(2,1)}, bf16[1,28,128,128]{3,2,1,0:T(8,128)(2,1)S(1)}, u32[]{:S(2)}, u32[]{:S(2)}) %collective-permute-start.6) | collective-permute-done | bytes 917536 | tf_op jit(solution)/shard_map/ppermute | solution.py:12
  138.6 18.6 %collective-permute-done.7 = bf16[1,28,128,128]{3,2,1,0:T(8,128)(2,1)S(1)} collective-permute-done((bf16[1,28,128,128]{3,2,1,0:T(8,128)(2,1)}, bf16[1,28,128,128]{3,2,1,0:T(8,128)(2,1)S(1)}, u32[]{:S(2)}, u32[]{:S(2)}) %collective-permute-start.7) | collective-permute-done | bytes 917536 | tf_op jit(solution)/shard_map/ppermute | solution.py:12
  157.3 3.2 copy-done
  160.5 138.8 %while.13 = (s32[]{:T(128)}, f32[4,28,128,128]{3,2,1,0:T(8,128)}, s32[4]{0:T(128)S(1)}, s32[]{:T(128)}, s32[256,28]{1,0:T(8,128)S(1)}, /*index=5*/s32[4,7]{1,0:T...) while((s32[]{:T(128)}, f32[4,28,128,128]{3,2,1,0:T(8,128)}, ...), condition=%wide.region_3.4_spmd.clone, body=%wide.region_0.3_spmd.clone.sunk | while | flops 825324992 | bytes 41536048 | solution.py:48
  164.7 11.4 %gather_fusion.1 = bf16[196,128,128]{2,1,0:T(8,128)(2,1)} fusion(bf16[252,128,128]{2,1,0:T(8,128)(2,1)} %get-tuple-element.282, s32[1024]{0:T(1024)S(1)} %pad_clamp_fusion.5), kind=kCustom, calls=%fused_computation.1.clone.clone.1 | custom fusion | bytes 12845840 | tf_op jit(solution)/shard_map/while/body/eval_jaxpr/gather | solution.py:45
  176.1 9.5 %copy.25 = bf16[7,28,128,128]{2,3,0,1:T(8,128)(2,1)} copy(bf16[7,28,128,128]{3,2,1,0:T(8,128)(2,1)} %bitcast.74) | data formatting | bytes 12845056 | tf_op jit(solution)/shard_map/while/body/eval_jaxpr/gather | solution.py:45
  186.0 5.9 %fusion.32 = f32[1,28,128,128]{2,3,1,0:T(8,128)} fusion(bf16[7,28,128,128]{2,3,0,1:T(8,128)(2,1)} %copy.25, pred[7,28]{0,1:T(8,128)(4,1)S(1)} %copy.26, bf16[4,7,128,128]{3,2,1,0:T(8,128)(2,1)} %get-tuple-element.283, s32[]{:T(128)S(6)} %select_n.153), kind=kOutput, calls=%fused_computation.7.clone.1 | convolution fusion | flops 825294848 | bytes 8487112 | tf_op jit(solution)/shard_map/while/body/eval_jaxpr/hab,hsbc->sac/dot_general | solution.py:46
  192.0 1.8 copy.27
  193.8 1.4 constant_dynamic-update-slice_fusion.2
  199.5 11.4 %gather_fusion.1 = bf16[196,128,128]{2,1,0:T(8,128)(2,1)} fusion(bf16[252,128,128]{2,1,0:T(8,128)(2,1)} %get-tuple-element.282, s32[1024]{0:T(1024)S(1)} %pad_clamp_fusion.5), kind=kCustom, calls=%fused_computation.1.clone.clone.1 | custom fusion | bytes 12845840 | tf_op jit(solution)/shard_map/while/body/eval_jaxpr/gather | solution.py:45
  210.9 9.5 %copy.25 = bf16[7,28,128,128]{2,3,0,1:T(8,128)(2,1)} copy(bf16[7,28,128,128]{3,2,1,0:T(8,128)(2,1)} %bitcast.74) | data formatting | bytes 12845056 | tf_op jit(solution)/shard_map/while/body/eval_jaxpr/gather | solution.py:45
  220.8 6.0 %fusion.32 = f32[1,28,128,128]{2,3,1,0:T(8,128)} fusion(bf16[7,28,128,128]{2,3,0,1:T(8,128)(2,1)} %copy.25, pred[7,28]{0,1:T(8,128)(4,1)S(1)} %copy.26, bf16[4,7,128,128]{3,2,1,0:T(8,128)(2,1)} %get-tuple-element.283, s32[]{:T(128)S(6)} %select_n.153), kind=kOutput, calls=%fused_computation.7.clone.1 | convolution fusion | flops 825294848 | bytes 8487112 | tf_op jit(solution)/shard_map/while/body/eval_jaxpr/hab,hsbc->sac/dot_general | solution.py:46
  226.7 1.8 copy.27
  234.1 11.4 %gather_fusion.1 = bf16[196,128,128]{2,1,0:T(8,128)(2,1)} fusion(bf16[252,128,128]{2,1,0:T(8,128)(2,1)} %get-tuple-element.282, s32[1024]{0:T(1024)S(1)} %pad_clamp_fusion.5), kind=kCustom, calls=%fused_computation.1.clone.clone.1 | custom fusion | bytes 12845840 | tf_op jit(solution)/shard_map/while/body/eval_jaxpr/gather | solution.py:45
  245.5 9.5 %copy.25 = bf16[7,28,128,128]{2,3,0,1:T(8,128)(2,1)} copy(bf16[7,28,128,128]{3,2,1,0:T(8,128)(2,1)} %bitcast.74) | data formatting | bytes 12845056 | tf_op jit(solution)/shard_map/while/body/eval_jaxpr/gather | solution.py:45
  255.4 5.9 %fusion.32 = f32[1,28,128,128]{2,3,1,0:T(8,128)} fusion(bf16[7,28,128,128]{2,3,0,1:T(8,128)(2,1)} %copy.25, pred[7,28]{0,1:T(8,128)(4,1)S(1)} %copy.26, bf16[4,7,128,128]{3,2,1,0:T(8,128)(2,1)} %get-tuple-element.283, s32[]{:T(128)S(6)} %select_n.153), kind=kOutput, calls=%fused_computation.7.clone.1 | convolution fusion | flops 825294848 | bytes 8487112 | tf_op jit(solution)/shard_map/while/body/eval_jaxpr/hab,hsbc->sac/dot_general | solution.py:46
  261.4 1.8 copy.27
  263.2 1.5 constant_dynamic-update-slice_fusion.2
  268.9 11.4 %gather_fusion.1 = bf16[196,128,128]{2,1,0:T(8,128)(2,1)} fusion(bf16[252,128,128]{2,1,0:T(8,128)(2,1)} %get-tuple-element.282, s32[1024]{0:T(1024)S(1)} %pad_clamp_fusion.5), kind=kCustom, calls=%fused_computation.1.clone.clone.1 | custom fusion | bytes 12845840 | tf_op jit(solution)/shard_map/while/body/eval_jaxpr/gather | solution.py:45
  280.3 9.5 %copy.25 = bf16[7,28,128,128]{2,3,0,1:T(8,128)(2,1)} copy(bf16[7,28,128,128]{3,2,1,0:T(8,128)(2,1)} %bitcast.74) | data formatting | bytes 12845056 | tf_op jit(solution)/shard_map/while/body/eval_jaxpr/gather | solution.py:45
  290.2 6.0 %fusion.32 = f32[1,28,128,128]{2,3,1,0:T(8,128)} fusion(bf16[7,28,128,128]{2,3,0,1:T(8,128)(2,1)} %copy.25, pred[7,28]{0,1:T(8,128)(4,1)S(1)} %copy.26, bf16[4,7,128,128]{3,2,1,0:T(8,128)(2,1)} %get-tuple-element.283, s32[]{:T(128)S(6)} %select_n.153), kind=kOutput, calls=%fused_computation.7.clone.1 | convolution fusion | flops 825294848 | bytes 8487112 | tf_op jit(solution)/shard_map/while/body/eval_jaxpr/hab,hsbc->sac/dot_general | solution.py:46
  296.1 1.8 copy.27
  300.1 75.0 %reduce-scatter.2.cloned.1.call-done = f32[1,28,128,128]{3,2,1,0:T(8,128)} async-done(((f32[4,28,128,128]{3,2,1,0:T(8,128)}), f32[1,28,128,128]{3,2,1,0:T(8,128)}) %reduce-scatter.2.cloned.1.call-update) | async-done | bytes 1835024 | tf_op jit(solution)/shard_map/reduce_scatter | solution.py:49
  375.1 3.5 multiply_add_fusion
  (79 shorter events, 18.7 us)
Async XLA Ops:
  7.2 103.3 %copy-start.2 = (bf16[1,28,128,128]{3,2,1,0:T(8,128)(2,1)S(1)}, bf16[1,28,128,128]{3,2,1,0:T(8,128)(2,1)}, u32[]{:S(2)}) copy-start(bf16[1,28,128,128]{3,2,1,0:T(8,128)(2,1)} %param.11) | copy-start | bytes 2752516
  7.2 367.9 %reduce-scatter.2.cloned.1.call-start = ((), (), s32[]{:S(2)}) async-start(), calls=%async_computation.1 | async-start | bytes 9175040 | tf_op jit(solution)/shard_map/reduce_scatter | solution.py:49
  7.2 37.0 %collective-permute-start = (bf16[1,28,128,128]{3,2,1,0:T(8,128)(2,1)}, bf16[1,28,128,128]{3,2,1,0:T(8,128)(2,1)}, u32[]{:S(2)}, u32[]{:S(2)}) collective-permute-start(bf16[1,28,128,128]{3,2,1,0:T(8,128)(2,1)} %param.11), channel_id=1, source_target_pairs={{240,0},{244,4},{248,8},{252,12},{0,16},{4,20},{8,24},{12,28},{16,... | collective-permute-start | bytes 2752520 | tf_op jit(solution)/shard_map/ppermute | solution.py:12
  11.1 75.6 %collective-permute-start.1 = (bf16[1,28,128,128]{3,2,1,0:T(8,128)(2,1)}, bf16[1,28,128,128]{3,2,1,0:T(8,128)(2,1)}, u32[]{:S(2)}, u32[]{:S(2)}) collective-permute-start(bf16[1,28,128,128]{3,2,1,0:T(8,128)(2,1)} %param.11), channel_id=1, source_target_pairs={{244,0},{248,4},{252,8},{0,12},{4,16},{8,20},{12,24},{16,28},{20,3... | collective-permute-start | bytes 2752520 | tf_op jit(solution)/shard_map/ppermute | solution.py:12
  16.2 89.5 %collective-permute-start.2 = (bf16[1,28,128,128]{3,2,1,0:T(8,128)(2,1)}, bf16[1,28,128,128]{3,2,1,0:T(8,128)(2,1)}, u32[]{:S(2)}, u32[]{:S(2)}) collective-permute-start(bf16[1,28,128,128]{3,2,1,0:T(8,128)(2,1)} %param.11), channel_id=1, source_target_pairs={{248,0},{252,4},{0,8},{4,12},{8,16},{12,20},{16,24},{20,28},{24,32... | collective-permute-start | bytes 2752520 | tf_op jit(solution)/shard_map/ppermute | solution.py:12
  16.9 93.4 %collective-permute-start.3 = (bf16[1,28,128,128]{3,2,1,0:T(8,128)(2,1)}, bf16[1,28,128,128]{3,2,1,0:T(8,128)(2,1)S(1)}, u32[]{:S(2)}, u32[]{:S(2)}) collective-permute-start(bf16[1,28,128,128]{3,2,1,0:T(8,128)(2,1)} %param.11), channel_id=1, source_target_pairs={{252,0},{0,4},{4,8},{8,12},{12,16},{16,20},{20,24},{24,28},{28,32}... | collective-permute-start | bytes 2752520 | tf_op jit(solution)/shard_map/ppermute | solution.py:12
  16.9 93.7 %collective-permute-start.4 = (bf16[1,28,128,128]{3,2,1,0:T(8,128)(2,1)}, bf16[1,28,128,128]{3,2,1,0:T(8,128)(2,1)S(1)}, u32[]{:S(2)}, u32[]{:S(2)}) collective-permute-start(bf16[1,28,128,128]{3,2,1,0:T(8,128)(2,1)} %param.11), channel_id=1, source_target_pairs={{4,0},{8,4},{12,8},{16,12},{20,16},{24,20},{28,24},{32,28},{36,32}... | collective-permute-start | bytes 2752520 | tf_op jit(solution)/shard_map/ppermute | solution.py:12
  44.3 66.5 %collective-permute-start.5 = (bf16[1,28,128,128]{3,2,1,0:T(8,128)(2,1)}, bf16[1,28,128,128]{3,2,1,0:T(8,128)(2,1)S(1)}, u32[]{:S(2)}, u32[]{:S(2)}) collective-permute-start(bf16[1,28,128,128]{3,2,1,0:T(8,128)(2,1)} %param.11), channel_id=1, source_target_pairs={{8,0},{12,4},{16,8},{20,12},{24,16},{28,20},{32,24},{36,28},{40,32... | collective-permute-start | bytes 2752520 | tf_op jit(solution)/shard_map/ppermute | solution.py:12
  61.7 98.7 %copy-start.4 = (s32[4,7]{1,0:T(4,128)S(1)}, s32[4,7]{1,0:T(4,128)}, u32[]{:S(2)}) copy-start(s32[4,7]{1,0:T(4,128)} %param.10) | copy-start | bytes 340
  86.8 51.7 %collective-permute-start.6 = (bf16[1,28,128,128]{3,2,1,0:T(8,128)(2,1)}, bf16[1,28,128,128]{3,2,1,0:T(8,128)(2,1)S(1)}, u32[]{:S(2)}, u32[]{:S(2)}) collective-permute-start(bf16[1,28,128,128]{3,2,1,0:T(8,128)(2,1)} %param.11), channel_id=1, source_target_pairs={{12,0},{16,4},{20,8},{24,12},{28,16},{32,20},{36,24},{40,28},{44,3... | collective-permute-start | bytes 2752520 | tf_op jit(solution)/shard_map/ppermute | solution.py:12
  105.7 51.5 %collective-permute-start.7 = (bf16[1,28,128,128]{3,2,1,0:T(8,128)(2,1)}, bf16[1,28,128,128]{3,2,1,0:T(8,128)(2,1)S(1)}, u32[]{:S(2)}, u32[]{:S(2)}) collective-permute-start(bf16[1,28,128,128]{3,2,1,0:T(8,128)(2,1)} %param.11), channel_id=1, source_target_pairs={{16,0},{20,4},{24,8},{28,12},{32,16},{36,20},{40,24},{44,28},{48,3... | collective-permute-start | bytes 2752520 | tf_op jit(solution)/shard_map/ppermute | solution.py:12
  157.3 3.2 copy-start
  299.3 75.8 %copy-start.1 = (f32[1,28,128,128]{3,2,1,0:T(8,128)S(1)}, f32[1,28,128,128]{3,2,1,0:T(8,128)}, u32[]{:S(2)}) copy-start(f32[1,28,128,128]{3,2,1,0:T(8,128)} %param.14) | copy-start | bytes 5505028
  299.3 75.8 %copy-start.3 = (bf16[1,28,128,128]{3,2,1,0:T(8,128)(2,1)S(1)}, bf16[1,28,128,128]{3,2,1,0:T(8,128)(2,1)}, u32[]{:S(2)}) copy-start(bf16[1,28,128,128]{3,2,1,0:T(8,128)(2,1)} %param.12) | copy-start | bytes 2752516
Sparse Core Ops, SparseCore 0:
  299.5 75.6 reduce-scatter.1
where the time goes:
time: 387 us; the launch traced here: 385 us
  waiting for transfers between devices  189 us (49%)
  local copies, waits for them, and re-layouts  110 us (28%)
  starting transfers between devices  30.6 us (8%)
  matrix products  23.8 us (6%)
  between operations  14.9 us (4%)
  loops' own time  10.6 us (3%)
  other arithmetic  6.2 us (2%)
    ppermute x8, waiting for transfers between devices, passed_along(): return lax.ppermute(block, axis, route)  114 us
    gather x8, local copies, waits for them, and re-layouts, row_term(): stacked[index]  83.5 us
    reduce_scatter x1, waiting for transfers between devices, shards(): lax.psum_scatter(partial_rows, 'layer', scatter_dimension=0, tiled=True)  75 us
    ppermute x8, starting transfers between devices, passed_along(): return lax.ppermute(block, axis, route)  30.6 us
    dot_general x4, matrix products, row_term(): jnp.einsum('hab,hsbc->sac', values, chosen, preferred_element_type=jnp.fl...  23.8 us
    dynamic_update_slice x8, local copies, waits for them, and re-layouts, shards(): partial_rows = lax.map(row_term, jnp.arange(group_rows, dtype=jnp.int32))  12.8 us
    another operation x1, loops' own time, shards(): partial_rows = lax.map(row_term, jnp.arange(group_rows, dtype=jnp.int32))  10.6 us
    unnamed x19, local copies, waits for them, and re-layouts  8.54 us
  transfers between devices with their start and end apart: 9, of which 7 were waited for; matrix products, arithmetic and copies ran while one was open for 1% of the time, Pallas kernels for 0%

commit v1 on v0

v1 whole, which is shorter than its diff:
```python
import functools

import jax
import jax.numpy as jnp
import numpy as np
from jax import lax
from jax.experimental import pallas as pl
from jax.experimental.pallas import tpu as pltpu
from jax.sharding import PartitionSpec as P

HW = 15
B = 128
K = 28
NB = 256
N_LAYER = 4
GROUP = 8
WIN = 4
EXTRA = 16
ROWS = WIN * B + EXTRA
NEAR = 24
FAR = 7
WIDE = 5
VMEM = 50 * 2**20


def halo_lists(step):
    far, near = [], []
    for cls in range(GROUP):
        got = {1: [], 2: []}
        for row in range(GROUP):
            for slot in range(WIN):
                col = cls + GROUP * (slot - 2 + (row > cls))
                if abs(col - row) > HW:
                    continue
                for dist in (1, 2):
                    at = GROUP * dist * step
                    if any(abs(out + at - row) <= HW and abs(out + at - col) <= HW for out in range(GROUP)):
                        got[dist].append(row * WIN + slot)
        assert set(got[2]) <= set(got[1])
        far.append(got[2])
        near.append([x for x in got[1] if x not in got[2]])
    return far, near


def table():
    lists = [*halo_lists(1), *halo_lists(-1)]
    sizes = [max(len(x) for x in part) for part in lists]
    rows = [sum(([*part[cls], *([-1] * (size - len(part[cls])))] for part, size in zip(lists, sizes)), []) for cls in range(GROUP)]
    return np.array(rows, np.int32), sizes


TABLE, SIZES = table()
STARTS = [sum(SIZES[:i]) for i in range(4)]


def whole(space=pltpu.VMEM):
    return pl.BlockSpec(memory_space=space)


def params():
    return pltpu.CompilerParams(vmem_limit_bytes=VMEM)


def window_place(col, own_row):
    ahead = (col - own_row + NB // 2) % NB - NB // 2 + 16
    return (own_row + ahead) % GROUP * WIN + ahead // GROUP


def spread_kernel(where_ref, t_ref, cols_ref, h_cols_ref, out_ref, cols, tile, sem):
    row = where_ref[0]
    base = pl.multiple_of(row // GROUP * GROUP, GROUP)
    copy = pltpu.make_async_copy(cols_ref.at[pl.ds(base, GROUP)], cols, sem)
    copy.start()
    tile[...] = jnp.zeros_like(tile)
    tile[0 : h_cols_ref.shape[0], 0 : h_cols_ref.shape[1]] = h_cols_ref[...].astype(jnp.float32)
    extra = tile[...].astype(jnp.bfloat16)
    for cls in range(GROUP):
        out_ref[cls, 0 : WIN * B, :] = jnp.zeros((WIN * B, B), jnp.bfloat16)
        out_ref[cls, WIN * B : ROWS, :] = extra
    copy.wait()
    for slot in range(K):
        place = window_place(cols[row % GROUP, slot], row)
        start = pl.multiple_of(place % WIN * B, B)
        out_ref[place // WIN, pl.ds(start, B), :] = t_ref[0, slot]


def spread(where, t_now, t_cols, h_cols):
    return pl.pallas_call(
        spread_kernel,
        out_shape=jax.ShapeDtypeStruct((GROUP, ROWS, B), jnp.bfloat16),
        in_specs=[whole(pltpu.SMEM), whole(), whole(pl.ANY), whole()],
        out_specs=whole(),
        scratch_shapes=[pltpu.SMEM((GROUP, K), jnp.int32), pltpu.VMEM((EXTRA, B), jnp.float32), pltpu.SemaphoreType.DMA],
        compiler_params=params(),
        name="spread",
    )(where, t_now, t_cols, h_cols)


def pack_kernel(where_ref, tab_ref, x_ref, *out_refs):
    cls = where_ref[1]
    for out_ref, first, size in zip(out_refs, STARTS, SIZES):
        for at in range(size):
            entry = jnp.maximum(tab_ref[cls, first + at], 0)
            start = pl.multiple_of(entry % WIN * B, B)
            out_ref[at] = x_ref[entry // WIN, pl.ds(start, B), :]


def pack(where, tab, x):
    return pl.pallas_call(
        pack_kernel,
        out_shape=[jax.ShapeDtypeStruct((size, B, B), jnp.bfloat16) for size in SIZES],
        in_specs=[whole(pltpu.SMEM), whole(pltpu.SMEM), whole()],
        out_specs=[whole()] * 4,
        compiler_params=params(),
        name="pack",
    )(where, tab, x)


def near_kernel(where_ref, tab_ref, hc_ref, x_ref, rf_ref, rn_ref, lf_ref, ln_ref, h_ref, acc_ref, far_ref, hd, xd):
    cls = where_ref[1]
    hd[...] = jnp.zeros_like(hd)
    far_ref[...] = jnp.zeros_like(far_ref)
    xd[...] = jnp.zeros_like(xd)

    @pl.loop(0, GROUP)
    def _(source):
        for r in range(N_LAYER):
            out_row = source // N_LAYER * N_LAYER + r
            start = pl.multiple_of(out_row * B, B)
            for slot in range(K // N_LAYER):
                at = hc_ref[source, r * (K // N_LAYER) + slot]
                block = h_ref[source, r, slot]
                is_near = jnp.logical_and(at >= GROUP, at < GROUP + NEAR)

                @pl.when(is_near)
                def _():
                    hd[at - GROUP, pl.ds(start, B), :] = block

                @pl.when(jnp.logical_not(is_near))
                def _():
                    far_ref[jnp.where(at < GROUP, at - 1, at - (GROUP + NEAR) + FAR), pl.ds(start, B), :] = block

    for row in range(GROUP):
        for slot in range(WIN):
            xd[slot + (row > cls).astype(jnp.int32), (GROUP + row) * B : (GROUP + row + 1) * B, :] = x_ref[row, slot * B : (slot + 1) * B, :]
    for ref, first, size, dist in zip((rf_ref, rn_ref, lf_ref, ln_ref), STARTS, SIZES, (-1, -1, 1, 1)):
        for at in range(size):
            entry = tab_ref[cls, first + at]
            row, slot = entry // WIN, entry % WIN
            col = slot + (row > cls).astype(jnp.int32) + dist
            start = jnp.where(entry >= 0, (GROUP * (1 + dist) + row) * B, NEAR * B)
            xd[jnp.clip(col, 0, WIDE - 1), pl.ds(pl.multiple_of(start, B), B), :] = ref[at]

    @pl.loop(0, 2)
    def _(half):
        rows = pl.ds(pl.multiple_of(half * (4 * B), 4 * B), 4 * B)
        left = jnp.concatenate([hd[n, rows, :] for n in range(NEAR)], axis=1)
        for col in range(0, WIDE, 2):
            wide = min(2, WIDE - col)
            right = jnp.concatenate([xd[col + i, 0 : NEAR * B, :] for i in range(wide)], axis=1)
            got = jnp.dot(left, right, preferred_element_type=jnp.float32)
            for i in range(wide):
                acc_ref[col + i, rows, :] = got[:, i * B : (i + 1) * B]


def near(where, tab, hc, x, rf, rn, lf, ln, h):
    return pl.pallas_call(
        near_kernel,
        out_shape=[
            jax.ShapeDtypeStruct((WIDE, GROUP * B, B), jnp.float32),
            jax.ShapeDtypeStruct((2 * FAR, GROUP * B, B), jnp.bfloat16),
        ],
        in_specs=[whole(pltpu.SMEM)] * 3 + [whole()] * 6,
        out_specs=[whole()] * 2,
        scratch_shapes=[pltpu.VMEM((NEAR, GROUP * B, B), jnp.bfloat16), pltpu.VMEM((WIDE, (NEAR + 1) * B, B), jnp.bfloat16)],
        compiler_params=params(),
        cost_estimate=pl.CostEstimate(flops=2 * 1024 * 3072 * 640, bytes_accessed=20_000_000, transcendentals=0),
        name="near",
    )(where, tab, hc, x, rf, rn, lf, ln, h)


def far_kernel(where_ref, tab_ref, acc_ref, far_ref, r_ref, l_ref, out_ref, xd, sums):
    cls = where_ref[1]
    xd[...] = jnp.zeros_like(xd)
    for side, (ref, first, size) in enumerate(((r_ref, STARTS[0], SIZES[0]), (l_ref, STARTS[2], SIZES[2]))):
        for at in range(size):
            entry = tab_ref[cls, first + at]
            row, slot = entry // WIN, entry % WIN
            col = slot + (row > cls).astype(jnp.int32) - (0 if side else 2)
            start = jnp.where(entry >= 0, (row if side else row - 1) * B, FAR * B)
            xd[side, jnp.clip(col, 0, 2), pl.ds(pl.multiple_of(start, B), B), :] = ref[at]

    @pl.loop(0, 2)
    def _(half):
        rows = pl.ds(pl.multiple_of(half * (4 * B), 4 * B), 4 * B)
        got = []
        for side in range(2):
            left = jnp.concatenate([far_ref[side * FAR + n, rows, :] for n in range(FAR)], axis=1)
            right = jnp.concatenate([xd[side, i, 0 : FAR * B, :] for i in range(3)], axis=1)
            got.append(jnp.dot(left, right, preferred_element_type=jnp.float32))
        for col in range(WIDE):
            total = acc_ref[col, rows, :]
            if col <= 2:
                total = total + got[0][:, col * B : (col + 1) * B]
            if col >= 2:
                total = total + got[1][:, (col - 2) * B : (col - 1) * B]
            sums[col, rows, :] = total.astype(jnp.bfloat16)

    for row in range(GROUP):
        for slot in range(WIN):
            out_ref[row, slot] = sums[slot + (row > cls).astype(jnp.int32), row * B : (row + 1) * B, :]


def far(where, tab, acc, far_h, fr, fl):
    return pl.pallas_call(
        far_kernel,
        out_shape=jax.ShapeDtypeStruct((GROUP, WIN, B, B), jnp.bfloat16),
        in_specs=[whole(pltpu.SMEM)] * 2 + [whole()] * 4,
        out_specs=whole(),
        scratch_shapes=[pltpu.VMEM((2, 3, (FAR + 1) * B, B), jnp.bfloat16), pltpu.VMEM((WIDE, GROUP * B, B), jnp.bfloat16)],
        compiler_params=params(),
        cost_estimate=pl.CostEstimate(flops=4 * 1024 * 896 * 384, bytes_accessed=8_000_000, transcendentals=0),
        name="far",
    )(where, tab, acc, far_h, fr, fl)


def update_kernel(where_ref, coef_ref, got_ref, cols_ref, prev_ref, density_ref, next_ref, out_ref, cols, sem):
    row = where_ref[0]
    step = pl.program_id(0)

    @pl.when(step == 0)
    def _():
        base = pl.multiple_of(row // GROUP * GROUP, GROUP)
        copy = pltpu.make_async_copy(cols_ref.at[pl.ds(base, GROUP)], cols, sem)
        copy.start()
        copy.wait()

    for i in range(4):
        place = window_place(cols[row % GROUP, step * 4 + i], row)
        product = got_ref[place // WIN, place % WIN].astype(jnp.float32)
        fresh = (2.0 * product - prev_ref[0, i].astype(jnp.float32)).astype(jnp.bfloat16)
        next_ref[0, i] = fresh
        out_ref[0, i] = density_ref[0, i] + coef_ref[0] * fresh.astype(jnp.float32)


def update(where, coefficient, got, t_cols, t_prev, density):
    blocks = pl.BlockSpec((1, 4, B, B), lambda i: (0, i, 0, 0))
    return pl.pallas_call(
        update_kernel,
        grid=(K // 4,),
        out_shape=[jax.ShapeDtypeStruct((1, K, B, B), jnp.bfloat16), jax.ShapeDtypeStruct((1, K, B, B), jnp.float32)],
        in_specs=[whole(pltpu.SMEM), whole(pltpu.SMEM), whole(), whole(pl.ANY), blocks, blocks],
        out_specs=[blocks, blocks],
        scratch_shapes=[pltpu.SMEM((GROUP, K), jnp.int32), pltpu.SemaphoreType.DMA],
        compiler_params=params(),
        name="update",
    )(where, coefficient, got, t_cols, t_prev, density)


def shards(h_vals, h_cols, t_now, t_prev, t_cols, density, coefficient):
    chips = lax.axis_size("grid") // 2
    groups = [[(2 * q + core) * N_LAYER + x for core in range(2) for x in range(N_LAYER)] for q in range(chips)]
    axes = ("grid", "layer")
    exchange = functools.partial(lax.all_to_all, axis_name=axes, split_axis=0, concat_axis=0, axis_index_groups=groups, tiled=True)

    def shift(block, step):
        count = lax.axis_size("grid")
        return lax.ppermute(block, "grid", [(i, (i + 2 * step) % count) for i in range(count)])

    grid_pos = lax.axis_index("grid")
    layer_pos = lax.axis_index("layer")
    own_row = grid_pos * N_LAYER + layer_pos
    where = jnp.stack([own_row, own_row % GROUP]).astype(jnp.int32)
    tab = jnp.asarray(TABLE)

    h_all = lax.all_gather(h_vals, axes, axis=0, axis_index_groups=groups)
    x = exchange(spread(where, t_now, t_cols, h_cols))
    hc = x[:, WIN * B : WIN * B + N_LAYER, 0 : K // N_LAYER].astype(jnp.int32)
    hc = ((hc - own_row // GROUP * GROUP + 2 * GROUP) % NB).reshape(GROUP, K)
    right_far, right_near, left_far, left_near = pack(where, tab, x)
    rf, lf = shift(right_far, 1), shift(left_far, -1)
    rn, ln = shift(right_near, 1), shift(left_near, -1)
    rff, lff = shift(rf, 1), shift(lf, -1)
    acc, far_h = near(where, tab, hc, x, rf, rn, lf, ln, h_all)
    sums = far(where, tab, acc, far_h, rff, lff)
    got = exchange(sums)
    return tuple(update(where, coefficient, got, t_cols, t_prev, density))


def solution(mesh):
    rows = P(("grid", "layer"), None, None, None)
    placed = (P("grid", "layer", None, None), P("grid", "layer"), rows, rows, P(), rows, P())
    return jax.shard_map(shards, mesh=mesh, in_specs=placed, out_specs=(rows, rows), check_vma=False)
```

time: 387 us -> 128 us (0.33)
  waiting for transfers between devices: 189 us -> 27.1 us
  local copies, waits for them, and re-layouts: 110 us -> 3.99 us
  Pallas kernels: 0 us -> 31.3 us
  blocking collectives: 0 us -> 24.7 us
  matrix products: 23.8 us -> 0 us
  loops' own time: 10.6 us -> 0 us
  other arithmetic: 6.2 us -> 0.1 us
  starting transfers between devices: 30.6 us -> 25.4 us
    ppermute x8 -> x6, waiting for transfers between devices: 114 us -> 12.1 us  [shift(): lax.ppermute(block, 'grid', [(i, (i + 2 * step) % count) for i in range(c...]
    gather x12 -> x0, local copies, waits for them, and re-layouts: 85.8 us -> none  [the longest x8 83.5 us: row_term(): stacked[index]]
    reduce_scatter x1 -> x0, waiting for transfers between devices: 75 us -> none  [shards(): lax.psum_scatter(partial_rows, 'layer', scatter_dimension=0, tiled=True)]
    pallas_call x0 -> x5, Pallas kernels: none -> 31.3 us  [the longest x1 16.6 us: near(): pl.pallas_call(near_kernel, out_shape=[jax.ShapeDtypeStruct((WIDE, GROUP...]
    all_to_all x0 -> x1, blocking collectives: none -> 24.7 us  [shards(): x = exchange(spread(where, t_now, t_cols, h_cols))]
    dot_general x4 -> x0, matrix products: 23.8 us -> none  [row_term(): jnp.einsum('hab,hsbc->sac', values, chosen, preferred_element_type=jnp.fl...]
    all_to_all x0 -> x1, waiting for transfers between devices: none -> 14.3 us  [shards(): got = exchange(sums)]
    dynamic_update_slice x8 -> x0, local copies, waits for them, and re-layouts: 12.8 us -> none  [shards(): partial_rows = lax.map(row_term, jnp.arange(group_rows, dtype=jnp.int32))]
  transfers between devices with their start and end apart: 9 -> 8, of which waited for: 7 -> 3; matrix products, arithmetic and copies ran while one was open for 1% -> 1% of each run, Pallas kernels for 0% -> 16%
where the time goes in v1:
time: 128 us; the launch traced here: 127 us
  Pallas kernels  31.3 us (24%)
  waiting for transfers between devices  27.1 us (21%)
  starting transfers between devices  25.4 us (20%)
  blocking collectives  24.7 us (19%)
  between operations  14.7 us (11%)
  local copies, waits for them, and re-layouts  3.99 us (3%)
    all_to_all x1, blocking collectives, shards(): x = exchange(spread(where, t_now, t_cols, h_cols))  24.7 us
    ppermute x6, starting transfers between devices, shift(): lax.ppermute(block, 'grid', [(i, (i + 2 * step) % count) for i in range(c...  20.4 us
    pallas_call x1, Pallas kernels, near(): pl.pallas_call(near_kernel, out_shape=[jax.ShapeDtypeStruct((WIDE, GROUP...  16.6 us
    all_to_all x1, waiting for transfers between devices, shards(): got = exchange(sums)  14.3 us
    ppermute x6, waiting for transfers between devices, shift(): lax.ppermute(block, 'grid', [(i, (i + 2 * step) % count) for i in range(c...  12.1 us
    pallas_call x1, Pallas kernels, far(): pl.pallas_call(far_kernel, out_shape=jax.ShapeDtypeStruct((GROUP, WIN, B,...  6.8 us
    all_to_all x1, starting transfers between devices, shards(): got = exchange(sums)  5.03 us
    pallas_call x1, Pallas kernels, update(): pl.pallas_call(update_kernel, grid=(K // 4,), out_shape=[jax.ShapeDtypeSt...  4.55 us
  transfers between devices with their start and end apart: 8, of which 3 were waited for; matrix products, arithmetic and copies ran while one was open for 1% of the time, Pallas kernels for 16%

profile of v1, /device:TPU:1, one launch (start us, length us, event | category | flops | bytes accessed | tf_op | source)
XLA Modules:
  0.0 127.4 jit_solution(4087959748348440439)
XLA Ops:
  7.2 0.0 all-gather.3.cloned.1.call-start
  7.2 0.7 all-gather.3.cloned.1.call-update
  7.9 0.9 copy.14.cols_ref
  8.8 0.1 pad_add_fusion.where_ref
  8.9 0.0 copy-start.1
  8.9 1.2 copy-done.1
  10.0 0.0 copy-start.4
  10.0 0.7 copy-done.4
  10.7 1.7 %spread.1 = bf16[8,528,128]{2,1,0:T(8,128)(2,1)S(1)} custom-call(s32[2]{0:T(128)S(1)} %pad_add_fusion.where_ref, bf16[1,28,128,128]{3,2,1,0:T(8,128)(2,1)S(1)} %copy-done.1, s32[256,28]{1,0:T(8,128)S(1)} %copy.14.cols_ref, s32[4,7]{1,0:T(4,128)S(1)} %copy-done.4), custom_call_target="tpu_custom_call" | custom-call | tf_op jit(solution)/shard_map/spread/pallas_call | solution.py:88
  12.5 24.7 %all_to_all.10.x_ref = bf16[8,528,128]{2,1,0:T(8,128)(2,1)S(1)} all-to-all(bf16[8,528,128]{2,1,0:T(8,128)(2,1)S(1)} %spread.1), channel_id=1, replica_groups={{0,1,2,3,4,5,6,7},{8,9,10,11,12,13,14,15},{16,17,18,19,20,21,22,23},{24..., dimensions={0} | all-to-all | bytes 2162688 | tf_op jit(solution)/shard_map/all_to_all | solution.py:277
  37.1 0.0 copy-done.3
  37.1 1.6 %pack.1 = (bf16[20,128,128]{2,1,0:T(8,128)(2,1)S(1)}, bf16[10,128,128]{2,1,0:T(8,128)(2,1)}, bf16[20,128,128]{2,1,0:T(8,128)(2,1)S(1)}, bf16[10,128,128]{2,1,0:T(8,128)(2,1)S(1)}) custom-call(s32[2]{0:T(128)S(1)} %pad_add_fusion.where_ref, s32[8,60]{1,0:T(8,128)S(1)} %copy-done.3, bf16[8,528,128]{2,1,0:T(8,128)(2,1)S(1)} %all_to_all.10.x_ref), custom_call_target="tpu_custom_call" | custom-call | tf_op jit(solution)/shard_map/pack/pallas_call | solution.py:109
  38.8 2.0 %collective-permute-start = (bf16[20,128,128]{2,1,0:T(8,128)(2,1)S(1)}, bf16[20,128,128]{2,1,0:T(8,128)(2,1)}, u32[]{:S(2)}, u32[]{:S(2)}) collective-permute-start(bf16[20,128,128]{2,1,0:T(8,128)(2,1)S(1)} %get-tuple-element.8), channel_id=1, source_target_pairs={{0,8},{4,12},{8,16},{12,20},{16,24},{20,28},{24,32},{28,36},{32,40... | collective-permute-start | bytes 1966088 | tf_op jit(solution)/shard_map/ppermute | solution.py:268
  40.7 8.8 %collective-permute-start.2 = (bf16[20,128,128]{2,1,0:T(8,128)(2,1)S(1)}, bf16[20,128,128]{2,1,0:T(8,128)(2,1)}, u32[]{:S(2)}, u32[]{:S(2)}) collective-permute-start(bf16[20,128,128]{2,1,0:T(8,128)(2,1)S(1)} %get-tuple-element.10), channel_id=1, source_target_pairs={{0,248},{4,252},{8,0},{12,4},{16,8},{20,12},{24,16},{28,20},{32,24... | collective-permute-start | bytes 1966088 | tf_op jit(solution)/shard_map/ppermute | solution.py:268
  49.6 0.0 collective-permute-start.1
  49.6 4.8 %collective-permute-start.3 = (bf16[10,128,128]{2,1,0:T(8,128)(2,1)S(1)}, bf16[10,128,128]{2,1,0:T(8,128)(2,1)}, u32[]{:S(2)}, u32[]{:S(2)}) collective-permute-start(bf16[10,128,128]{2,1,0:T(8,128)(2,1)S(1)} %get-tuple-element.11), channel_id=1, source_target_pairs={{0,248},{4,252},{8,0},{12,4},{16,8},{20,12},{24,16},{28,20},{32,24... | collective-permute-start | bytes 983048 | tf_op jit(solution)/shard_map/ppermute | solution.py:268
  54.4 10.1 %collective-permute-done.rf_ref = bf16[20,128,128]{2,1,0:T(8,128)(2,1)} collective-permute-done((bf16[20,128,128]{2,1,0:T(8,128)(2,1)S(1)}, bf16[20,128,128]{2,1,0:T(8,128)(2,1)}, u32[]{:S(2)}, u32[]{:S(2)}) %collective-permute-start) | collective-permute-done | bytes 655392 | tf_op jit(solution)/shard_map/ppermute | solution.py:268
  64.5 0.0 collective-permute-start.4
  64.5 0.0 collective-permute-done.2.lf_ref
  64.5 4.8 %collective-permute-start.5 = (bf16[20,128,128]{2,1,0:T(8,128)(2,1)}, bf16[20,128,128]{2,1,0:T(8,128)(2,1)S(1)}, u32[]{:S(2)}, u32[]{:S(2)}) collective-permute-start(bf16[20,128,128]{2,1,0:T(8,128)(2,1)} %collective-permute-done.2.lf_ref), channel_id=1, source_target_pairs={{0,248},{4,252},{8,0},{12,4},{16,8},{20,12},{24,16},{28,20},{32,24... | collective-permute-start | bytes 1966088 | tf_op jit(solution)/shard_map/ppermute | solution.py:268
  69.3 0.1 reshape.7.hc_ref
  69.3 2.0 %collective-permute-done.1.rn_ref = bf16[10,128,128]{2,1,0:T(8,128)(2,1)S(1)} collective-permute-done((bf16[10,128,128]{2,1,0:T(8,128)(2,1)}, bf16[10,128,128]{2,1,0:T(8,128)(2,1)S(1)}, u32[]{:S(2)}, u32[]{:S(2)}) %collective-permute-start.1) | collective-permute-done | bytes 327712 | tf_op jit(solution)/shard_map/ppermute | solution.py:268
  71.4 0.0 collective-permute-done.3.ln_ref
  71.4 16.6 %near.1 = (f32[5,1024,128]{2,1,0:T(8,128)}, bf16[14,1024,128]{2,1,0:T(8,128)(2,1)}) custom-call(s32[2]{0:T(128)S(1)} %pad_add_fusion.where_ref, s32[8,60]{1,0:T(8,128)S(1)} %copy-done.3, s32[8,28]{1,0:T(8,128)S(1)} %reshape.7.hc_ref, bf16[8,528,128]{2,1,0:T(8,128)(2,1)S(1)} %all_to_all.10.x_ref, bf16[20,128,128]{2,1,0:T(8,128)(2,1)} %collective-permute-done.rf_ref, ...), custom_call_target="tpu_custom_call" | custom-call | flops 4026531840 | bytes 20000000 | tf_op jit(solution)/shard_map/near/pallas_call | solution.py:167
  88.0 0.0 collective-permute-done.4.r_ref
  88.0 0.0 collective-permute-done.5.l_ref
  88.0 6.8 %far.1 = bf16[8,4,128,128]{3,2,1,0:T(8,128)(2,1)} custom-call(s32[2]{0:T(128)S(1)} %pad_add_fusion.where_ref, s32[8,60]{1,0:T(8,128)S(1)} %copy-done.3, f32[5,1024,128]{2,1,0:T(8,128)} %get-tuple-element.12.acc_ref, bf16[14,1024,128]{2,1,0:T(8,128)(2,1)} %get-tuple-element.13.far_ref, bf16[20,128,128]{2,1,0:T(8,128)(2,1)S(1)} %collective-permute-done.4.r_ref, ...), custom_call_target="tpu_custom_call" | custom-call | flops 1409286144 | bytes 8000000 | tf_op jit(solution)/shard_map/far/pallas_call | solution.py:215
  94.8 5.0 %all-to-all-start.1 = ((bf16[8,4,128,128]{3,2,1,0:T(8,128)(2,1)}), bf16[8,4,128,128]{3,2,1,0:T(8,128)(2,1)S(1)}, u32[]{:S(2)}, u32[]{:S(2)}) async-start(bf16[8,4,128,128]{3,2,1,0:T(8,128)(2,1)} %far.1), calls=%async_computation.1 | async-start | bytes 2097152 | tf_op jit(solution)/shard_map/all_to_all | solution.py:286
  100.5 14.3 %all-to-all-done.1.got_ref = bf16[8,4,128,128]{3,2,1,0:T(8,128)(2,1)S(1)} async-done(((bf16[8,4,128,128]{3,2,1,0:T(8,128)(2,1)}), bf16[8,4,128,128]{3,2,1,0:T(8,128)(2,1)S(1)}, u32[]{:S(2)}, u32[]{:S(2)}) %all-to-all-start.1) | async-done | bytes 1048608 | tf_op jit(solution)/shard_map/all_to_all | solution.py:286
  114.8 0.0 copy-done
  114.8 1.2 copy-done.2
  116.0 4.5 %update.1 = (bf16[1,28,128,128]{3,2,1,0:T(8,128)(2,1)}, f32[1,28,128,128]{3,2,1,0:T(8,128)}) custom-call(s32[2]{0:T(128)S(1)} %pad_add_fusion.where_ref, f32[1]{0:T(128)S(6)} %copy.16.coef_ref, bf16[8,4,128,128]{3,2,1,0:T(8,128)(2,1)S(1)} %all-to-all-done.1.got_ref, s32[256,28]{1,0:T(8,128)S(1)} %copy.14.cols_ref, bf16[1,28,128,128]{3,2,1,0:T(8,128)(2,1)S(1)} %copy-done.2, ...), custom_call_target="tpu_custom_call" | custom-call | tf_op jit(solution)/shard_map/update/pallas_call | solution.py:248
  (5 shorter events, 0.0 us)
Async XLA Ops:
  7.2 64.2 %all-gather.3.cloned.1.call-start = ((), (), s32[]{:S(2)}) async-start(), calls=%async_computation.2 | async-start | bytes 8257536 | tf_op jit(solution)/shard_map/all_gather | solution.py:276
  8.9 1.2 copy-start.1
  10.0 0.7 copy-start.4
  10.7 26.4 %copy-start.3 = (s32[8,60]{1,0:T(8,128)S(1)}, s32[8,60]{1,0:T(8,128)}, u32[]{:S(2)}) copy-start(s32[8,60]{1,0:T(8,128)} %constant.55.clone.tab_ref) | copy-start | bytes 5764
  38.8 25.7 %collective-permute-start = (bf16[20,128,128]{2,1,0:T(8,128)(2,1)S(1)}, bf16[20,128,128]{2,1,0:T(8,128)(2,1)}, u32[]{:S(2)}, u32[]{:S(2)}) collective-permute-start(bf16[20,128,128]{2,1,0:T(8,128)(2,1)S(1)} %get-tuple-element.8), channel_id=1, source_target_pairs={{0,8},{4,12},{8,16},{12,20},{16,24},{20,28},{24,32},{28,36},{32,40... | collective-permute-start | bytes 1966088 | tf_op jit(solution)/shard_map/ppermute | solution.py:268
  40.7 23.7 %collective-permute-start.2 = (bf16[20,128,128]{2,1,0:T(8,128)(2,1)S(1)}, bf16[20,128,128]{2,1,0:T(8,128)(2,1)}, u32[]{:S(2)}, u32[]{:S(2)}) collective-permute-start(bf16[20,128,128]{2,1,0:T(8,128)(2,1)S(1)} %get-tuple-element.10), channel_id=1, source_target_pairs={{0,248},{4,252},{8,0},{12,4},{16,8},{20,12},{24,16},{28,20},{32,24... | collective-permute-start | bytes 1966088 | tf_op jit(solution)/shard_map/ppermute | solution.py:268
  49.6 21.8 %collective-permute-start.1 = (bf16[10,128,128]{2,1,0:T(8,128)(2,1)}, bf16[10,128,128]{2,1,0:T(8,128)(2,1)S(1)}, u32[]{:S(2)}, u32[]{:S(2)}) collective-permute-start(bf16[10,128,128]{2,1,0:T(8,128)(2,1)} %get-tuple-element.9), channel_id=1, source_target_pairs={{0,8},{4,12},{8,16},{12,20},{16,24},{20,28},{24,32},{28,36},{32,40... | collective-permute-start | bytes 983048 | tf_op jit(solution)/shard_map/ppermute | solution.py:268
  49.6 21.8 %collective-permute-start.3 = (bf16[10,128,128]{2,1,0:T(8,128)(2,1)S(1)}, bf16[10,128,128]{2,1,0:T(8,128)(2,1)}, u32[]{:S(2)}, u32[]{:S(2)}) collective-permute-start(bf16[10,128,128]{2,1,0:T(8,128)(2,1)S(1)} %get-tuple-element.11), channel_id=1, source_target_pairs={{0,248},{4,252},{8,0},{12,4},{16,8},{20,12},{24,16},{28,20},{32,24... | collective-permute-start | bytes 983048 | tf_op jit(solution)/shard_map/ppermute | solution.py:268
  64.5 23.5 %collective-permute-start.4 = (bf16[20,128,128]{2,1,0:T(8,128)(2,1)}, bf16[20,128,128]{2,1,0:T(8,128)(2,1)S(1)}, u32[]{:S(2)}, u32[]{:S(2)}) collective-permute-start(bf16[20,128,128]{2,1,0:T(8,128)(2,1)} %collective-permute-done.rf_ref), channel_id=1, source_target_pairs={{0,8},{4,12},{8,16},{12,20},{16,24},{20,28},{24,32},{28,36},{32,40... | collective-permute-start | bytes 1966088 | tf_op jit(solution)/shard_map/ppermute | solution.py:268
  64.5 23.5 %collective-permute-start.5 = (bf16[20,128,128]{2,1,0:T(8,128)(2,1)}, bf16[20,128,128]{2,1,0:T(8,128)(2,1)S(1)}, u32[]{:S(2)}, u32[]{:S(2)}) collective-permute-start(bf16[20,128,128]{2,1,0:T(8,128)(2,1)} %collective-permute-done.2.lf_ref), channel_id=1, source_target_pairs={{0,248},{4,252},{8,0},{12,4},{16,8},{20,12},{24,16},{28,20},{32,24... | collective-permute-start | bytes 1966088 | tf_op jit(solution)/shard_map/ppermute | solution.py:268
  94.8 20.0 %copy-start = (f32[1,28,128,128]{3,2,1,0:T(8,128)S(1)}, f32[1,28,128,128]{3,2,1,0:T(8,128)}, u32[]{:S(2)}) copy-start(f32[1,28,128,128]{3,2,1,0:T(8,128)} %density_ref.1) | copy-start | bytes 5505028
  94.8 20.0 %all-to-all-start.1 = ((bf16[8,4,128,128]{3,2,1,0:T(8,128)(2,1)}), bf16[8,4,128,128]{3,2,1,0:T(8,128)(2,1)S(1)}, u32[]{:S(2)}, u32[]{:S(2)}) async-start(bf16[8,4,128,128]{3,2,1,0:T(8,128)(2,1)} %far.1), calls=%async_computation.1 | async-start | bytes 2097152 | tf_op jit(solution)/shard_map/all_to_all | solution.py:286
  114.8 1.2 copy-start.2
Sparse Core Ops, SparseCore 0:
  9.9 55.2 all-gather.2

commit v2 on v1

v2 whole, which is shorter than its diff:
```python
import functools

import jax
import jax.numpy as jnp
import numpy as np
from jax import lax
from jax.experimental import pallas as pl
from jax.experimental.pallas import tpu as pltpu
from jax.sharding import PartitionSpec as P

HW = 15
B = 128
K = 28
NB = 256
N_LAYER = 4
GROUP = 8
WIN = 4
EXTRA = 16
ROWS = WIN * B + EXTRA
NEAR = 24
FAR = 7
WIDE = 5
MIB = 2**20


def halo_lists(step):
    far, near = [], []
    for cls in range(GROUP):
        got = {1: [], 2: []}
        for row in range(GROUP):
            for slot in range(WIN):
                col = cls + GROUP * (slot - 2 + (row > cls))
                if abs(col - row) > HW:
                    continue
                for dist in (1, 2):
                    at = GROUP * dist * step
                    if any(abs(out + at - row) <= HW and abs(out + at - col) <= HW for out in range(GROUP)):
                        got[dist].append(row * WIN + slot)
        assert set(got[2]) <= set(got[1])
        far.append(got[2])
        near.append([x for x in got[1] if x not in got[2]])
    return far, near


def table():
    lists = [*halo_lists(1), *halo_lists(-1)]
    sizes = [max(len(x) for x in part) for part in lists]
    rows = [sum(([*part[cls], *([-1] * (size - len(part[cls])))] for part, size in zip(lists, sizes)), []) for cls in range(GROUP)]
    return np.array(rows, np.int32), sizes


TABLE, SIZES = table()
STARTS = [sum(SIZES[:i]) for i in range(4)]


def whole(space=pltpu.VMEM):
    return pl.BlockSpec(memory_space=space)


def in_hbm(x):
    return pltpu.with_memory_space_constraint(x, pltpu.HBM)


def params(mib):
    return pltpu.CompilerParams(vmem_limit_bytes=mib * MIB)


def absent(present_at, size):
    every = jnp.arange(size, dtype=jnp.int32)
    missing = jnp.all(present_at[..., None, :] != every[:, None], axis=-1)
    rank = jnp.sum(jnp.where(every[None, :] < every[:, None], missing[..., None, :], False).astype(jnp.int32), axis=-1)
    wanted = jnp.arange(size - present_at.shape[-1], dtype=jnp.int32)
    hit = jnp.logical_and(missing[..., None, :], rank[..., None, :] == wanted[:, None])
    return jnp.sum(jnp.where(hit, every, 0), axis=-1)


def spread_kernel(where_ref, t_ref, cols_ref, h_cols_ref, out_ref, places_ref, cols, tile, cols_sem, sem):
    row = where_ref[0]
    half = pl.multiple_of(row // B * B, B)
    load = pltpu.make_async_copy(cols_ref.at[:, pl.ds(half, B)], cols, cols_sem)
    load.start()
    tile[...] = jnp.zeros_like(tile)
    tile[0 : h_cols_ref.shape[0], 0 : h_cols_ref.shape[1]] = h_cols_ref[...].astype(jnp.float32)
    for cls in range(GROUP):
        out_ref[cls, 0 : WIN * B, :] = jnp.zeros((WIN * B, B), jnp.bfloat16)
        out_ref[cls, WIN * B : ROWS, :] = tile[...].astype(jnp.bfloat16)
    load.wait()
    for slot in range(K):
        ahead = (cols[slot, row % B] - row + NB // 2) % NB - NB // 2 + 2 * GROUP
        place = (row + ahead) % GROUP * WIN + ahead // GROUP
        places_ref[slot] = place
        start = pl.multiple_of(place % WIN * B, B)
        pltpu.make_async_copy(t_ref.at[0, slot], out_ref.at[place // WIN, pl.ds(start, B)], sem).start()
    pltpu.make_async_copy(t_ref, t_ref, sem).wait()


def spread(where, t_now, t_cols, h_cols):
    return pl.pallas_call(
        spread_kernel,
        out_shape=[jax.ShapeDtypeStruct((GROUP, ROWS, B), jnp.bfloat16), jax.ShapeDtypeStruct((K,), jnp.int32)],
        in_specs=[whole(pltpu.SMEM), whole(pltpu.HBM), whole(pltpu.HBM), whole()],
        out_specs=[whole(), whole(pltpu.SMEM)],
        scratch_shapes=[
            pltpu.SMEM((K, B), jnp.int32),
            pltpu.VMEM((EXTRA, B), jnp.float32),
            pltpu.SemaphoreType.DMA,
            pltpu.SemaphoreType.DMA,
        ],
        compiler_params=params(8),
        name="spread",
    )(where, in_hbm(t_now), in_hbm(t_cols.T), h_cols)


def pack_kernel(parts, where_ref, tab_ref, x_ref, *refs):
    out_refs = refs[(len(refs) - len(parts)) // 2 :][: len(parts)]
    cls = where_ref[1]
    for out_ref, part in zip(out_refs, parts):
        for at in range(SIZES[part]):
            entry = jnp.maximum(tab_ref[cls, STARTS[part] + at], 0)
            start = pl.multiple_of(entry % WIN * B, B)
            out_ref[at] = x_ref[entry // WIN, pl.ds(start, B), :]


def pack(where, tab, x, parts, held):
    return pl.pallas_call(
        functools.partial(pack_kernel, parts),
        out_shape=[jax.ShapeDtypeStruct((SIZES[part], B, B), jnp.bfloat16) for part in parts]
        + [jax.ShapeDtypeStruct(h.shape, h.dtype) for h in held],
        in_specs=[whole(pltpu.SMEM), whole(pltpu.SMEM), whole()] + [whole(pltpu.HBM)] * len(held),
        out_specs=[whole()] * len(parts) + [whole(pltpu.HBM)] * len(held),
        input_output_aliases={3 + i: len(parts) + i for i in range(len(held))},
        compiler_params=params(8),
        name="pack",
    )(where, tab, x, *map(in_hbm, held))


def merge_kernel(first_ref, second_ref, out_ref, sems):
    half = first_ref.shape[0]
    copies = [pltpu.make_async_copy(ref, out_ref.at[i * half : (i + 1) * half], sems.at[i]) for i, ref in enumerate((first_ref, second_ref))]
    for copy in copies:
        copy.start()
    for copy in copies:
        copy.wait()


def merge(first, second):
    return pl.pallas_call(
        merge_kernel,
        out_shape=jax.ShapeDtypeStruct((2 * first.shape[0], *first.shape[1:]), first.dtype),
        in_specs=[whole(pltpu.HBM)] * 2,
        out_specs=whole(pltpu.HBM),
        scratch_shapes=[pltpu.SemaphoreType.DMA((2,))],
        compiler_params=params(4),
        name="merge",
    )(in_hbm(first), in_hbm(second))


def after_kernel(*_):
    pass


def after(held, *first):
    return pl.pallas_call(
        after_kernel,
        out_shape=jax.ShapeDtypeStruct(held.shape, held.dtype),
        in_specs=[whole(pltpu.HBM)] + [whole(pl.ANY)] * len(first),
        out_specs=whole(pltpu.HBM),
        input_output_aliases={0: 0},
        compiler_params=params(4),
        name="after",
    )(in_hbm(held), *first)


H_PARTS = (((0, 0),), ((0, 1),), ((-1, 0),), ((1, 1),), ((-1, 1), (2, 0)), ((1, 0), (2, 1)))


def near_kernel(where_ref, tab_ref, h_at_ref, x_ref, rf_ref, rn_ref, lf_ref, ln_ref, *refs):
    *h_refs, acc_ref, far_ref, hd, xd, sem = refs
    cls = where_ref[1]

    own_core = cls // N_LAYER
    for h_ref, parts in zip(h_refs, H_PARTS):
        for number, (apart, other) in enumerate(parts):
            core = 1 - own_core if other else own_core
            layer = (cls + apart * (1 - 2 * own_core) + N_LAYER) % N_LAYER

            @pl.loop(0, N_LAYER)
            def _(r):
                out_row = core * N_LAYER + r
                rows = pl.ds(pl.multiple_of(out_row * B, B), B)
                for slot in range(K // N_LAYER):
                    at = h_at_ref[out_row, layer * (K // N_LAYER) + slot]
                    pltpu.make_async_copy(h_ref.at[number * N_LAYER + r, slot], hd.at[at, rows], sem).start()

    @pl.loop(0, GROUP)
    def _(out_row):
        rows = pl.ds(pl.multiple_of(out_row * B, B), B)
        for i in range(K, NEAR + GROUP):
            hd[h_at_ref[out_row, i], rows, :] = jnp.zeros((B, B), jnp.bfloat16)

    xd[...] = jnp.zeros_like(xd)
    for row in range(GROUP):
        for slot in range(WIN):
            xd[slot + (row > cls).astype(jnp.int32), (GROUP + row) * B : (GROUP + row + 1) * B, :] = x_ref[row, slot * B : (slot + 1) * B, :]
    for ref, first, size, dist in zip((rf_ref, rn_ref, lf_ref, ln_ref), STARTS, SIZES, (-1, -1, 1, 1)):
        for i in range(size):
            entry = tab_ref[cls, first + i]
            row, slot = entry // WIN, entry % WIN
            col = slot + (row > cls).astype(jnp.int32) + dist
            start = jnp.where(entry >= 0, (GROUP * (1 + dist) + row) * B, NEAR * B)
            xd[jnp.clip(col, 0, WIDE - 1), pl.ds(pl.multiple_of(start, B), B), :] = ref[i]
    pltpu.make_async_copy(hd.at[0:K], hd.at[0:K], sem).wait()

    @pl.loop(0, GROUP)
    def _(out_row):
        rows = pl.ds(pl.multiple_of(out_row * B, B), B)
        for i in range(GROUP):
            far_ref[i, rows, :] = hd[NEAR + i, rows, :]
        shift = (out_row > cls).astype(jnp.int32)
        left = jnp.concatenate([hd[n, rows, :] for n in range(NEAR)], axis=1)
        for slot in range(0, WIN, 2):
            right = jnp.concatenate([xd[slot + i + shift, 0 : NEAR * B, :] for i in range(2)], axis=1)
            got = jnp.dot(left, right, preferred_element_type=jnp.float32)
            for i in range(2):
                acc_ref[out_row, slot + i] = got[:, i * B : (i + 1) * B]


def near(where, tab, h_at, x, rf, rn, lf, ln, h_parts):
    return pl.pallas_call(
        near_kernel,
        out_shape=[
            jax.ShapeDtypeStruct((GROUP, WIN, B, B), jnp.float32),
            jax.ShapeDtypeStruct((GROUP, GROUP * B, B), jnp.bfloat16),
        ],
        in_specs=[whole(pltpu.SMEM)] * 3 + [whole()] * 5 + [whole(pltpu.HBM)] * len(h_parts),
        out_specs=[whole()] * 2,
        scratch_shapes=[
            pltpu.VMEM((NEAR + GROUP, GROUP * B, B), jnp.bfloat16),
            pltpu.VMEM((WIDE, (NEAR + 1) * B, B), jnp.bfloat16),
            pltpu.SemaphoreType.DMA,
        ],
        compiler_params=params(30),
        cost_estimate=pl.CostEstimate(flops=2 * 1024 * 3072 * 512, bytes_accessed=20_000_000, transcendentals=0),
        name="near",
    )(where, tab, h_at, x, rf, rn, lf, ln, *map(in_hbm, h_parts))


def far_kernel(where_ref, tab_ref, acc_ref, far_ref, r_ref, l_ref, out_ref, xd):
    cls = where_ref[1]
    xd[...] = jnp.zeros_like(xd)
    for ref, first, size, dist in ((r_ref, STARTS[0], SIZES[0], -2), (l_ref, STARTS[2], SIZES[2], 2)):
        for i in range(size):
            entry = tab_ref[cls, first + i]
            row, slot = entry // WIN, entry % WIN
            col = slot + (row > cls).astype(jnp.int32) + dist
            start = jnp.where(entry >= 0, (GROUP * (dist // 2 + 1) // 2 + row) * B, 2 * GROUP * B)
            xd[jnp.clip(col, 0, WIDE - 1), pl.ds(pl.multiple_of(start, B), B), :] = ref[i]

    @pl.loop(0, GROUP)
    def _(out_row):
        first = pl.multiple_of(out_row * B, B)
        shift = (out_row > cls).astype(jnp.int32)
        left = jnp.concatenate([far_ref[n, pl.ds(first, B), :] for n in range(GROUP)], axis=1)
        for slot in range(0, WIN, 2):
            right = jnp.concatenate([xd[slot + i + shift, pl.ds(first, GROUP * B), :] for i in range(2)], axis=1)
            got = jnp.dot(left, right, preferred_element_type=jnp.float32)
            for i in range(2):
                out_ref[out_row, slot + i] = (acc_ref[out_row, slot + i] + got[:, i * B : (i + 1) * B]).astype(jnp.bfloat16)


def far(where, tab, acc, far_h, fr, fl):
    return pl.pallas_call(
        far_kernel,
        out_shape=jax.ShapeDtypeStruct((GROUP, WIN, B, B), jnp.bfloat16),
        in_specs=[whole(pltpu.SMEM)] * 2 + [whole()] * 4,
        out_specs=whole(),
        scratch_shapes=[pltpu.VMEM((WIDE, (2 * GROUP + 1) * B, B), jnp.bfloat16)],
        compiler_params=params(16),
        cost_estimate=pl.CostEstimate(flops=2 * 1024 * 1024 * 512, bytes_accessed=8_000_000, transcendentals=0),
        name="far",
    )(where, tab, acc, far_h, fr, fl)


CHUNK = 4


def update_kernel(places_ref, coef_ref, got_ref, density_ref, prev_hbm, next_hbm, out_hbm, prev, fresh, out, prev_sem, next_sem, out_sem):
    def at(ref, part):
        return ref.at[0, part * CHUNK : (part + 1) * CHUNK]

    def copies(part):
        return (
            pltpu.make_async_copy(at(prev_hbm, part), at(prev, part), prev_sem.at[part]),
            pltpu.make_async_copy(at(fresh, part), at(next_hbm, part), next_sem.at[part]),
            pltpu.make_async_copy(at(out, part), at(out_hbm, part), out_sem.at[part]),
        )

    for part in range(K // CHUNK):
        copies(part)[0].start()
    for part in range(K // CHUNK):
        load, *stores = copies(part)
        load.wait()
        for slot in range(part * CHUNK, (part + 1) * CHUNK):
            place = places_ref[slot]
            product = got_ref[place // WIN, place % WIN].astype(jnp.float32)
            value = (2.0 * product - prev[0, slot].astype(jnp.float32)).astype(jnp.bfloat16)
            fresh[0, slot] = value
            out[0, slot] = density_ref[0, slot] + coef_ref[0] * value.astype(jnp.float32)
        for store in stores:
            store.start()
    for part in range(K // CHUNK):
        copies(part)[1].wait()
        copies(part)[2].wait()


def update(places, coefficient, got, density, t_prev):
    shape = (1, K, B, B)
    sems = pltpu.SemaphoreType.DMA((K // CHUNK,))
    return pl.pallas_call(
        update_kernel,
        out_shape=[jax.ShapeDtypeStruct(shape, jnp.bfloat16), jax.ShapeDtypeStruct(shape, jnp.float32)],
        in_specs=[whole(pltpu.SMEM), whole(pltpu.SMEM), whole(), whole(), whole(pltpu.HBM)],
        out_specs=[whole(pltpu.HBM)] * 2,
        scratch_shapes=[pltpu.VMEM(shape, jnp.bfloat16), pltpu.VMEM(shape, jnp.bfloat16), pltpu.VMEM(shape, jnp.float32), sems, sems, sems],
        compiler_params=params(16),
        name="update",
    )(places, coefficient, got, density, in_hbm(t_prev))


def shards(h_vals, h_cols, t_now, t_prev, t_cols, density, coefficient):
    chips = lax.axis_size("grid") // 2
    groups = [[(2 * q + core) * N_LAYER + x for core in range(2) for x in range(N_LAYER)] for q in range(chips)]
    axes = ("grid", "layer")
    exchange = functools.partial(lax.all_to_all, axis_name=axes, split_axis=0, concat_axis=0, axis_index_groups=groups, tiled=True)

    def shift(block, step):
        count = lax.axis_size("grid")
        return lax.ppermute(block, "grid", [(i, (i + 2 * step) % count) for i in range(count)])

    def along(block):
        route = [(g * N_LAYER + x, g * N_LAYER + (x + 1 - 2 * (g % 2)) % N_LAYER) for g in range(2 * chips) for x in range(N_LAYER)]
        return lax.ppermute(block, axes, route)

    def across(block):
        return lax.ppermute(block, "grid", [(i, i ^ 1) for i in range(2 * chips)])

    own_row = lax.axis_index("grid") * N_LAYER + lax.axis_index("layer")
    where = jnp.stack([own_row, own_row % GROUP]).astype(jnp.int32)
    tab = jnp.asarray(TABLE)

    h_one, h_other = along(h_vals), across(h_vals)
    spread_t, places = spread(where, t_now, t_cols, h_cols)
    x = exchange(spread_t)
    held = (h_one, h_other, across(h_one), merge(h_other, h_one))
    right_far, left_far, right_near, left_near, h_one, h_other, h_back, h_next = pack(where, tab, x, (0, 2, 1, 3), held)
    rf, lf = shift(right_far, 1), shift(left_far, -1)
    rn, ln = shift(right_near, 1), shift(left_near, -1)
    h_next = after(along(h_next), rf, lf, rn, ln)
    h_parts = [h_vals, h_other, h_one, h_back, h_next, across(h_next)]
    h_at = x[:, WIN * B : WIN * B + N_LAYER, 0 : K // N_LAYER].astype(jnp.int32)
    h_at = (h_at - own_row // GROUP * GROUP + 2 * GROUP) % NB
    h_at = h_at.reshape(2, N_LAYER, N_LAYER, K // N_LAYER).transpose(0, 2, 1, 3).reshape(GROUP, K)
    out_rows = jnp.arange(GROUP, dtype=jnp.int32)[:, None]
    is_near = jnp.logical_and(h_at >= GROUP, h_at < GROUP + NEAR)
    h_at = jnp.where(is_near, h_at - GROUP, NEAR + (h_at - out_rows) % GROUP)
    h_at = jnp.concatenate([h_at, absent(h_at, NEAR + GROUP)], axis=1)
    rff, lff = shift(rf, 1), shift(lf, -1)
    acc, far_h = near(where, tab, h_at, x, rf, rn, lf, ln, h_parts)
    sums = far(where, tab, acc, far_h, rff, lff)
    got = exchange(sums)
    return tuple(update(places, coefficient, got, density, t_prev))


def solution(mesh):
    rows = P(("grid", "layer"), None, None, None)
    placed = (P("grid", "layer", None, None), P("grid", "layer"), rows, rows, P(), rows, P())
    return jax.shard_map(shards, mesh=mesh, in_specs=placed, out_specs=(rows, rows), check_vma=False)
```

time: 128 us -> 116 us (0.906)
  blocking collectives: 24.7 us -> 0 us
  starting transfers between devices: 25.4 us -> 41.2 us
  waiting for transfers between devices: 27.1 us -> 42.7 us
  between operations: 14.7 us -> 1.56 us
  Pallas kernels: 31.3 us -> 23.1 us
  local copies, waits for them, and re-layouts: 3.99 us -> 6.37 us
    all_to_all x1 -> x0, blocking collectives: 24.7 us -> none  [shards(): x = exchange(spread(where, t_now, t_cols, h_cols))]
    ppermute x0 -> x5, starting transfers between devices: none -> 14.5 us  [the longest x3 11 us: across(): return lax.ppermute(block, 'grid', [(i, i ^ 1) for i in range(2 * chips)])]
    ppermute x6, waiting for transfers between devices: 12.1 us -> 26 us  [shift(): lax.ppermute(block, 'grid', [(i, (i + 2 * step) % count) for i in range(c...]
    pallas_call x4 -> x6, Pallas kernels: 24.5 us -> 18.3 us  [the longest x1 8.91 us: near(): pl.pallas_call(near_kernel, out_shape=[jax.ShapeDtypeStruct((GROUP, WIN,...]
    all_to_all x0 -> x1, starting transfers between devices: none -> 4.45 us  [shards(): x = exchange(spread_t)]
    ppermute x6, starting transfers between devices: 20.4 us -> 17.5 us  [shift(): lax.ppermute(block, 'grid', [(i, (i + 2 * step) % count) for i in range(c...]
    unnamed x11 -> x20, local copies, waits for them, and re-layouts: 3.91 us -> 6.1 us
    ppermute x0 -> x5, waiting for transfers between devices: none -> 2.03 us  [the longest x2 2.02 us: along(): return lax.ppermute(block, axes, route)]
  transfers between devices with their start and end apart: 8 -> 13, of which waited for: 3 -> 6; matrix products, arithmetic and copies ran while one was open for 1% -> 1% of each run, Pallas kernels for 16% -> 12%
where the time goes in v2:
time: 116 us
  waiting for transfers between devices  42.7 us (37%)
  starting transfers between devices  41.2 us (36%)
  Pallas kernels  23.1 us (20%)
  local copies, waits for them, and re-layouts  6.37 us (5%)
  between operations  1.56 us (1%)
    ppermute x6, waiting for transfers between devices, shift(): lax.ppermute(block, 'grid', [(i, (i + 2 * step) % count) for i in range(c...  26 us
    ppermute x6, starting transfers between devices, shift(): lax.ppermute(block, 'grid', [(i, (i + 2 * step) % count) for i in range(c...  17.5 us
    all_to_all x1, waiting for transfers between devices, shards(): got = exchange(sums)  14.3 us
    ppermute x3, starting transfers between devices, across(): return lax.ppermute(block, 'grid', [(i, i ^ 1) for i in range(2 * chips)])  11 us
    pallas_call x1, Pallas kernels, near(): pl.pallas_call(near_kernel, out_shape=[jax.ShapeDtypeStruct((GROUP, WIN,...  8.91 us
    unnamed x20, local copies, waits for them, and re-layouts  6.1 us
    pallas_call x1, Pallas kernels, far(): pl.pallas_call(far_kernel, out_shape=jax.ShapeDtypeStruct((GROUP, WIN, B,...  4.8 us
    all_to_all x1, starting transfers between devices, shards(): got = exchange(sums)  4.72 us
  transfers between devices with their start and end apart: 13, of which 6 were waited for; matrix products, arithmetic and copies ran while one was open for 1% of the time, Pallas kernels for 12%

profile of v2, /device:TPU:1, one launch (start us, length us, event | category | flops | bytes accessed | tf_op | source)
XLA Modules:
  0.0 115.6 jit_solution(3294858316518239299)
XLA Ops:
  0.6 3.4 %collective-permute-start = (bf16[4,7,128,128]{3,2,1,0:T(8,128)(2,1)}, bf16[4,7,128,128]{3,2,1,0:T(8,128)(2,1)S(1)}, u32[]{:S(2)}, u32[]{:S(2)}) collective-permute-start(bf16[4,7,128,128]{3,2,1,0:T(8,128)(2,1)} %refs_0_.1), channel_id=1, source_target_pairs={{0,1},{1,2},{2,3},{3,0},{4,7},{5,4},{6,5},{7,6},{8,9},{9,10},{10,1... | collective-permute-start | bytes 2752520 | tf_op jit(solution)/shard_map/ppermute | solution.py:342
  4.1 0.7 copy-done.5
  4.8 3.8 %spread.1 = (bf16[8,528,128]{2,1,0:T(8,128)(2,1)}, s32[28]{0:T(128)S(1)}) custom-call(s32[2]{0:T(128)S(1)} %pad_add_fusion.1.where_ref, bf16[1,28,128,128]{3,2,1,0:T(8,128)(2,1)} %t_ref.1, s32[28,256]{1,0:T(8,128)} %bitcast.7, s32[4,7]{1,0:T(4,128)S(1)} %copy-done.5), custom_call_target="tpu_custom_call" | custom-call | tf_op jit(solution)/shard_map/spread/pallas_call | solution.py:98
  8.6 4.5 %all-to-all-start = ((bf16[8,528,128]{2,1,0:T(8,128)(2,1)}), bf16[8,528,128]{2,1,0:T(8,128)(2,1)S(1)}, u32[]{:S(2)}, u32[]{:S(2)}) async-start(bf16[8,528,128]{2,1,0:T(8,128)(2,1)} %get-tuple-element.15), calls=%async_computation | async-start | bytes 2162688 | tf_op jit(solution)/shard_map/all_to_all | solution.py:353
  13.1 0.1 collective-permute-start.1
  13.2 2.0 %collective-permute-done.second_ref.refs_0_ = bf16[4,7,128,128]{3,2,1,0:T(8,128)(2,1)S(1)} collective-permute-done((bf16[4,7,128,128]{3,2,1,0:T(8,128)(2,1)}, bf16[4,7,128,128]{3,2,1,0:T(8,128)(2,1)S(1)}, u32[]{:S(2)}, u32[]{:S(2)}) %collective-permute-start) | collective-permute-done | bytes 917536 | tf_op jit(solution)/shard_map/ppermute | solution.py:342
  15.2 10.5 %collective-permute-start.2 = (bf16[4,7,128,128]{3,2,1,0:T(8,128)(2,1)S(1)}, bf16[4,7,128,128]{3,2,1,0:T(8,128)(2,1)S(1)}, u32[]{:S(2)}, u32[]{:S(2)}) collective-permute-start(bf16[4,7,128,128]{3,2,1,0:T(8,128)(2,1)S(1)} %collective-permute-done.second_ref.refs_0_), channel_id=1, source_target_pairs={{0,4},{4,0},{8,12},{12,8},{16,20},{20,16},{24,28},{28,24},{32,36},... | collective-permute-start | bytes 2752520 | tf_op jit(solution)/shard_map/ppermute | solution.py:345
  25.7 0.9 copy-done.7
  26.7 1.5 %merge.1.refs_3_ = bf16[8,7,128,128]{3,2,1,0:T(8,128)(2,1)S(1)} custom-call(bf16[4,7,128,128]{3,2,1,0:T(8,128)(2,1)} %copy-done.7, bf16[4,7,128,128]{3,2,1,0:T(8,128)(2,1)} %copy-done.6), custom_call_target="tpu_custom_call" | custom-call | tf_op jit(solution)/shard_map/merge/pallas_call | solution.py:147
  28.2 1.2 %copy-done = bf16[8,7,128,128]{3,2,1,0:T(8,128)(2,1)} copy-done((bf16[8,7,128,128]{3,2,1,0:T(8,128)(2,1)}, bf16[8,7,128,128]{3,2,1,0:T(8,128)(2,1)S(1)}, u32[]{:S(2)}) %copy-start) | copy-done | bytes 1835032
  29.4 0.3 all-to-all-done.x_ref
  29.7 0.9 copy-done.9
  30.6 0.9 pack.1
  31.6 1.2 %collective-permute-start.3 = (bf16[20,128,128]{2,1,0:T(8,128)(2,1)S(1)}, bf16[20,128,128]{2,1,0:T(8,128)(2,1)S(1)}, u32[]{:S(2)}, u32[]{:S(2)}) collective-permute-start(bf16[20,128,128]{2,1,0:T(8,128)(2,1)S(1)} %get-tuple-element.16), channel_id=1, source_target_pairs={{0,8},{4,12},{8,16},{12,20},{16,24},{20,28},{24,32},{28,36},{32,40... | collective-permute-start | bytes 1966088 | tf_op jit(solution)/shard_map/ppermute | solution.py:338
  32.8 6.4 %collective-permute-start.5 = (bf16[20,128,128]{2,1,0:T(8,128)(2,1)S(1)}, bf16[20,128,128]{2,1,0:T(8,128)(2,1)}, u32[]{:S(2)}, u32[]{:S(2)}) collective-permute-start(bf16[20,128,128]{2,1,0:T(8,128)(2,1)S(1)} %get-tuple-element.18), channel_id=1, source_target_pairs={{0,248},{4,252},{8,0},{12,4},{16,8},{20,12},{24,16},{28,20},{32,24... | collective-permute-start | bytes 1966088 | tf_op jit(solution)/shard_map/ppermute | solution.py:338
  39.2 4.8 %collective-permute-start.6 = (bf16[10,128,128]{2,1,0:T(8,128)(2,1)S(1)}, bf16[10,128,128]{2,1,0:T(8,128)(2,1)S(1)}, u32[]{:S(2)}, u32[]{:S(2)}) collective-permute-start(bf16[10,128,128]{2,1,0:T(8,128)(2,1)S(1)} %get-tuple-element.19), channel_id=1, source_target_pairs={{0,248},{4,252},{8,0},{12,4},{16,8},{20,12},{24,16},{28,20},{32,24... | collective-permute-start | bytes 983048 | tf_op jit(solution)/shard_map/ppermute | solution.py:338
  44.0 17.2 %collective-permute-done.4.__3_.rn_ref = bf16[10,128,128]{2,1,0:T(8,128)(2,1)S(1)} collective-permute-done((bf16[10,128,128]{2,1,0:T(8,128)(2,1)S(1)}, bf16[10,128,128]{2,1,0:T(8,128)(2,1)S(1)}, u32[]{:S(2)}, u32[]{:S(2)}) %collective-permute-start.4) | collective-permute-done | bytes 327712 | tf_op jit(solution)/shard_map/ppermute | solution.py:338
  61.3 1.3 %copy-done.8 = bf16[8,7,128,128]{3,2,1,0:T(8,128)(2,1)} copy-done((bf16[8,7,128,128]{3,2,1,0:T(8,128)(2,1)}, bf16[8,7,128,128]{3,2,1,0:T(8,128)(2,1)S(1)}, u32[]{:S(2)}) %copy-start.8) | copy-done | bytes 1835032
  62.6 0.4 collective-permute-start.8
  63.1 0.1 copy.17
  63.2 5.1 %collective-permute-start.10 = (bf16[20,128,128]{2,1,0:T(8,128)(2,1)}, bf16[20,128,128]{2,1,0:T(8,128)(2,1)S(1)}, u32[]{:S(2)}, u32[]{:S(2)}) collective-permute-start(bf16[20,128,128]{2,1,0:T(8,128)(2,1)} %collective-permute-done.5.__2_.lf_ref), channel_id=1, source_target_pairs={{0,248},{4,252},{8,0},{12,4},{16,8},{20,12},{24,16},{28,20},{32,24... | collective-permute-start | bytes 1966088 | tf_op jit(solution)/shard_map/ppermute | solution.py:338
  68.3 0.1 fusion
  68.4 0.2 convert_reduce_fusion
  68.6 0.1 select_reduce_fusion
  69.0 1.0 copy-done.3
  69.9 8.9 %near.1 = (f32[8,4,128,128]{3,2,1,0:T(8,128)S(1)}, bf16[8,1024,128]{2,1,0:T(8,128)(2,1)S(1)}) custom-call(s32[2]{0:T(128)S(1)} %pad_add_fusion.1.where_ref, s32[8,60]{1,0:T(8,128)S(1)} %copy-done.4, s32[8,32]{1,0:T(8,128)S(1)} %pad_add_fusion.h_at_ref, bf16[8,528,128]{2,1,0:T(8,128)(2,1)S(1)} %all-to-all-done.x_ref, ...), custom_call_target="tpu_custom_call" | custom-call | flops 3221225472 | bytes 20000000 | tf_op jit(solution)/shard_map/near/pallas_call | solution.py:229
  78.9 3.9 %collective-permute-done.10.l_ref = bf16[20,128,128]{2,1,0:T(8,128)(2,1)S(1)} collective-permute-done((bf16[20,128,128]{2,1,0:T(8,128)(2,1)}, bf16[20,128,128]{2,1,0:T(8,128)(2,1)S(1)}, u32[]{:S(2)}, u32[]{:S(2)}) %collective-permute-start.10) | collective-permute-done | bytes 655392 | tf_op jit(solution)/shard_map/ppermute | solution.py:338
  82.8 4.9 %collective-permute-done.9.r_ref = bf16[20,128,128]{2,1,0:T(8,128)(2,1)S(1)} collective-permute-done((bf16[20,128,128]{2,1,0:T(8,128)(2,1)S(1)}, bf16[20,128,128]{2,1,0:T(8,128)(2,1)S(1)}, u32[]{:S(2)}, u32[]{:S(2)}) %collective-permute-start.9) | collective-permute-done | bytes 655392 | tf_op jit(solution)/shard_map/ppermute | solution.py:338
  87.7 4.8 %far.1 = bf16[8,4,128,128]{3,2,1,0:T(8,128)(2,1)} custom-call(s32[2]{0:T(128)S(1)} %pad_add_fusion.1.where_ref, s32[8,60]{1,0:T(8,128)S(1)} %copy-done.4, f32[8,4,128,128]{3,2,1,0:T(8,128)S(1)} %get-tuple-element.24.acc_ref, bf16[8,1024,128]{2,1,0:T(8,128)(2,1)S(1)} %get-tuple-element.25.far_ref, bf16[20,128,128]{2,1,0:T(8,128)(2,1)S(1)} %collective-permute-done.9.r_ref, ...), custom_call_target="tpu_custom_call" | custom-call | flops 1073741824 | bytes 8000000 | tf_op jit(solution)/shard_map/far/pallas_call | solution.py:272
  92.5 4.7 %all-to-all-start.1 = ((bf16[8,4,128,128]{3,2,1,0:T(8,128)(2,1)}), bf16[8,4,128,128]{3,2,1,0:T(8,128)(2,1)S(1)}, u32[]{:S(2)}, u32[]{:S(2)}) async-start(bf16[8,4,128,128]{3,2,1,0:T(8,128)(2,1)} %far.1), calls=%async_computation.1 | async-start | bytes 2097152 | tf_op jit(solution)/shard_map/all_to_all | solution.py:370
  97.8 14.3 %all-to-all-done.1.got_ref = bf16[8,4,128,128]{3,2,1,0:T(8,128)(2,1)S(1)} async-done(((bf16[8,4,128,128]{3,2,1,0:T(8,128)(2,1)}), bf16[8,4,128,128]{3,2,1,0:T(8,128)(2,1)S(1)}, u32[]{:S(2)}, u32[]{:S(2)}) %all-to-all-start.1) | async-done | bytes 1048608 | tf_op jit(solution)/shard_map/all_to_all | solution.py:370
  112.2 3.2 %update.1 = (bf16[1,28,128,128]{3,2,1,0:T(8,128)(2,1)}, f32[1,28,128,128]{3,2,1,0:T(8,128)}) custom-call(s32[28]{0:T(128)S(1)} %get-tuple-element.14.places_ref, f32[1]{0:T(128)S(6)} %copy.24.coef_ref, bf16[8,4,128,128]{3,2,1,0:T(8,128)(2,1)S(1)} %all-to-all-done.1.got_ref, f32[1,28,128,128]{3,2,1,0:T(8,128)S(1)} %copy-done.1, bf16[1,28,128,128]{3,2,1,0:T(8,128)(2,1)} %prev_hbm.1), custom_call_target="tpu_custom_call" | custom-call | tf_op jit(solution)/shard_map/update/pallas_call | solution.py:319
  (33 shorter events, 0.6 us)
Async XLA Ops:
  0.6 14.6 %collective-permute-start = (bf16[4,7,128,128]{3,2,1,0:T(8,128)(2,1)}, bf16[4,7,128,128]{3,2,1,0:T(8,128)(2,1)S(1)}, u32[]{:S(2)}, u32[]{:S(2)}) collective-permute-start(bf16[4,7,128,128]{3,2,1,0:T(8,128)(2,1)} %refs_0_.1), channel_id=1, source_target_pairs={{0,1},{1,2},{2,3},{3,0},{4,7},{5,4},{6,5},{7,6},{8,9},{9,10},{10,1... | collective-permute-start | bytes 2752520 | tf_op jit(solution)/shard_map/ppermute | solution.py:342
  4.1 0.7 copy-start.5
  8.6 21.0 %all-to-all-start = ((bf16[8,528,128]{2,1,0:T(8,128)(2,1)}), bf16[8,528,128]{2,1,0:T(8,128)(2,1)S(1)}, u32[]{:S(2)}, u32[]{:S(2)}) async-start(bf16[8,528,128]{2,1,0:T(8,128)(2,1)} %get-tuple-element.15), calls=%async_computation | async-start | bytes 2162688 | tf_op jit(solution)/shard_map/all_to_all | solution.py:353
  13.1 17.5 %copy-start.4 = (s32[8,60]{1,0:T(8,128)S(1)}, s32[8,60]{1,0:T(8,128)}, u32[]{:S(2)}) copy-start(s32[8,60]{1,0:T(8,128)} %constant.77.clone.tab_ref) | copy-start | bytes 5764
  13.1 12.7 %collective-permute-start.1 = (bf16[4,7,128,128]{3,2,1,0:T(8,128)(2,1)}, bf16[4,7,128,128]{3,2,1,0:T(8,128)(2,1)S(1)}, u32[]{:S(2)}, u32[]{:S(2)}) collective-permute-start(bf16[4,7,128,128]{3,2,1,0:T(8,128)(2,1)} %refs_0_.1), channel_id=1, source_target_pairs={{0,4},{4,0},{8,12},{12,8},{16,20},{20,16},{24,28},{28,24},{32,36},... | collective-permute-start | bytes 2752520 | tf_op jit(solution)/shard_map/ppermute | solution.py:345
  15.2 10.6 %copy-start.6 = (bf16[4,7,128,128]{3,2,1,0:T(8,128)(2,1)}, bf16[4,7,128,128]{3,2,1,0:T(8,128)(2,1)S(1)}, u32[]{:S(2)}) copy-start(bf16[4,7,128,128]{3,2,1,0:T(8,128)(2,1)S(1)} %collective-permute-done.second_ref.refs_0_) | copy-start | bytes 2752516
  15.2 14.5 %collective-permute-start.2 = (bf16[4,7,128,128]{3,2,1,0:T(8,128)(2,1)S(1)}, bf16[4,7,128,128]{3,2,1,0:T(8,128)(2,1)S(1)}, u32[]{:S(2)}, u32[]{:S(2)}) collective-permute-start(bf16[4,7,128,128]{3,2,1,0:T(8,128)(2,1)S(1)} %collective-permute-done.second_ref.refs_0_), channel_id=1, source_target_pairs={{0,4},{4,0},{8,12},{12,8},{16,20},{20,16},{24,28},{28,24},{32,36},... | collective-permute-start | bytes 2752520 | tf_op jit(solution)/shard_map/ppermute | solution.py:345
  25.7 0.9 copy-start.7
  28.2 1.2 %copy-start = (bf16[8,7,128,128]{3,2,1,0:T(8,128)(2,1)}, bf16[8,7,128,128]{3,2,1,0:T(8,128)(2,1)S(1)}, u32[]{:S(2)}) copy-start(bf16[8,7,128,128]{3,2,1,0:T(8,128)(2,1)S(1)} %merge.1.refs_3_) | copy-start | bytes 5505028
  29.7 0.9 copy-start.9
  31.5 29.7 %collective-permute-start.7 = (bf16[8,7,128,128]{3,2,1,0:T(8,128)(2,1)}, bf16[8,7,128,128]{3,2,1,0:T(8,128)(2,1)S(1)}, u32[]{:S(2)}, u32[]{:S(2)}) collective-permute-start(bf16[8,7,128,128]{3,2,1,0:T(8,128)(2,1)} %get-tuple-element.23), channel_id=1, source_target_pairs={{0,1},{1,2},{2,3},{3,0},{4,7},{5,4},{6,5},{7,6},{8,9},{9,10},{10,1... | collective-permute-start | bytes 5505032 | tf_op jit(solution)/shard_map/ppermute | solution.py:342
  31.6 29.6 %collective-permute-start.3 = (bf16[20,128,128]{2,1,0:T(8,128)(2,1)S(1)}, bf16[20,128,128]{2,1,0:T(8,128)(2,1)S(1)}, u32[]{:S(2)}, u32[]{:S(2)}) collective-permute-start(bf16[20,128,128]{2,1,0:T(8,128)(2,1)S(1)} %get-tuple-element.16), channel_id=1, source_target_pairs={{0,8},{4,12},{8,16},{12,20},{16,24},{20,28},{24,32},{28,36},{32,40... | collective-permute-start | bytes 1966088 | tf_op jit(solution)/shard_map/ppermute | solution.py:338
  32.8 28.4 %collective-permute-start.5 = (bf16[20,128,128]{2,1,0:T(8,128)(2,1)S(1)}, bf16[20,128,128]{2,1,0:T(8,128)(2,1)}, u32[]{:S(2)}, u32[]{:S(2)}) collective-permute-start(bf16[20,128,128]{2,1,0:T(8,128)(2,1)S(1)} %get-tuple-element.18), channel_id=1, source_target_pairs={{0,248},{4,252},{8,0},{12,4},{16,8},{20,12},{24,16},{28,20},{32,24... | collective-permute-start | bytes 1966088 | tf_op jit(solution)/shard_map/ppermute | solution.py:338
  39.2 22.0 %collective-permute-start.4 = (bf16[10,128,128]{2,1,0:T(8,128)(2,1)S(1)}, bf16[10,128,128]{2,1,0:T(8,128)(2,1)S(1)}, u32[]{:S(2)}, u32[]{:S(2)}) collective-permute-start(bf16[10,128,128]{2,1,0:T(8,128)(2,1)S(1)} %get-tuple-element.17), channel_id=1, source_target_pairs={{0,8},{4,12},{8,16},{12,20},{16,24},{20,28},{24,32},{28,36},{32,40... | collective-permute-start | bytes 983048 | tf_op jit(solution)/shard_map/ppermute | solution.py:338
  39.2 22.0 %collective-permute-start.6 = (bf16[10,128,128]{2,1,0:T(8,128)(2,1)S(1)}, bf16[10,128,128]{2,1,0:T(8,128)(2,1)S(1)}, u32[]{:S(2)}, u32[]{:S(2)}) collective-permute-start(bf16[10,128,128]{2,1,0:T(8,128)(2,1)S(1)} %get-tuple-element.19), channel_id=1, source_target_pairs={{0,248},{4,252},{8,0},{12,4},{16,8},{20,12},{24,16},{28,20},{32,24... | collective-permute-start | bytes 983048 | tf_op jit(solution)/shard_map/ppermute | solution.py:338
  61.2 1.4 %copy-start.2 = (bf16[10,128,128]{2,1,0:T(8,128)(2,1)}, bf16[10,128,128]{2,1,0:T(8,128)(2,1)S(1)}, u32[]{:S(2)}) copy-start(bf16[10,128,128]{2,1,0:T(8,128)(2,1)S(1)} %collective-permute-done.6.__4_.ln_ref) | copy-start | bytes 983044
  61.2 1.3 %copy-start.8 = (bf16[8,7,128,128]{3,2,1,0:T(8,128)(2,1)}, bf16[8,7,128,128]{3,2,1,0:T(8,128)(2,1)S(1)}, u32[]{:S(2)}) copy-start(bf16[8,7,128,128]{3,2,1,0:T(8,128)(2,1)S(1)} %collective-permute-done.7.__0_) | copy-start | bytes 5505028
  62.6 6.3 %collective-permute-start.8 = (bf16[8,7,128,128]{3,2,1,0:T(8,128)(2,1)}, bf16[8,7,128,128]{3,2,1,0:T(8,128)(2,1)}, u32[]{:S(2)}, u32[]{:S(2)}) collective-permute-start(bf16[8,7,128,128]{3,2,1,0:T(8,128)(2,1)} %after.1.refs_4_), channel_id=1, source_target_pairs={{0,4},{4,0},{8,12},{12,8},{16,20},{20,16},{24,28},{28,24},{32,36},... | collective-permute-start | bytes 5505032 | tf_op jit(solution)/shard_map/ppermute | solution.py:345
  63.2 19.5 %collective-permute-start.10 = (bf16[20,128,128]{2,1,0:T(8,128)(2,1)}, bf16[20,128,128]{2,1,0:T(8,128)(2,1)S(1)}, u32[]{:S(2)}, u32[]{:S(2)}) collective-permute-start(bf16[20,128,128]{2,1,0:T(8,128)(2,1)} %collective-permute-done.5.__2_.lf_ref), channel_id=1, source_target_pairs={{0,248},{4,252},{8,0},{12,4},{16,8},{20,12},{24,16},{28,20},{32,24... | collective-permute-start | bytes 1966088 | tf_op jit(solution)/shard_map/ppermute | solution.py:338
  68.3 19.4 %collective-permute-start.9 = (bf16[20,128,128]{2,1,0:T(8,128)(2,1)S(1)}, bf16[20,128,128]{2,1,0:T(8,128)(2,1)S(1)}, u32[]{:S(2)}, u32[]{:S(2)}) collective-permute-start(bf16[20,128,128]{2,1,0:T(8,128)(2,1)S(1)} %collective-permute-done.3.__1_.rf_ref), channel_id=1, source_target_pairs={{0,8},{4,12},{8,16},{12,20},{16,24},{20,28},{24,32},{28,36},{32,40... | collective-permute-start | bytes 1966088 | tf_op jit(solution)/shard_map/ppermute | solution.py:338
  68.9 1.0 copy-start.3
  92.5 19.7 %copy-start.1 = (f32[1,28,128,128]{3,2,1,0:T(8,128)S(1)}, f32[1,28,128,128]{3,2,1,0:T(8,128)}, u32[]{:S(2)}) copy-start(f32[1,28,128,128]{3,2,1,0:T(8,128)} %density_ref.1) | copy-start | bytes 5505028
  92.5 19.7 %all-to-all-start.1 = ((bf16[8,4,128,128]{3,2,1,0:T(8,128)(2,1)}), bf16[8,4,128,128]{3,2,1,0:T(8,128)(2,1)S(1)}, u32[]{:S(2)}, u32[]{:S(2)}) async-start(bf16[8,4,128,128]{3,2,1,0:T(8,128)(2,1)} %far.1), calls=%async_computation.1 | async-start | bytes 2097152 | tf_op jit(solution)/shard_map/all_to_all | solution.py:370

commit v3 on v2

--- a/solution.py
+++ b/solution.py
@@ -74,101 +74,106 @@
     return jnp.sum(jnp.where(hit, every, 0), axis=-1)
 
 
-def spread_kernel(where_ref, t_ref, cols_ref, h_cols_ref, out_ref, places_ref, cols, tile, cols_sem, sem):
+def spread_kernel(where_ref, t_ref, cols_ref, h_cols_ref, out_ref, places_ref, cols, h_cols, tile, sems):
     row = where_ref[0]
     half = pl.multiple_of(row // B * B, B)
-    load = pltpu.make_async_copy(cols_ref.at[:, pl.ds(half, B)], cols, cols_sem)
-    load.start()
+    load_cols = pltpu.make_async_copy(cols_ref.at[:, pl.ds(half, B)], cols, sems.at[0])
+    load_h_cols = pltpu.make_async_copy(h_cols_ref, h_cols, sems.at[1])
+    load_cols.start()
+    load_h_cols.start()
     tile[...] = jnp.zeros_like(tile)
-    tile[0 : h_cols_ref.shape[0], 0 : h_cols_ref.shape[1]] = h_cols_ref[...].astype(jnp.float32)
     for cls in range(GROUP):
         out_ref[cls, 0 : WIN * B, :] = jnp.zeros((WIN * B, B), jnp.bfloat16)
-        out_ref[cls, WIN * B : ROWS, :] = tile[...].astype(jnp.bfloat16)
-    load.wait()
+    load_cols.wait()
     for slot in range(K):
         ahead = (cols[slot, row % B] - row + NB // 2) % NB - NB // 2 + 2 * GROUP
         place = (row + ahead) % GROUP * WIN + ahead // GROUP
         places_ref[slot] = place
         start = pl.multiple_of(place % WIN * B, B)
-        pltpu.make_async_copy(t_ref.at[0, slot], out_ref.at[place // WIN, pl.ds(start, B)], sem).start()
-    pltpu.make_async_copy(t_ref, t_ref, sem).wait()
+        pltpu.make_async_copy(t_ref.at[0, slot], out_ref.at[place // WIN, pl.ds(start, B)], sems.at[2]).start()
+    load_h_cols.wait()
+    tile[0 : h_cols.shape[0], 0 : h_cols.shape[1]] = h_cols[...].astype(jnp.float32)
+    for cls in range(GROUP):
+        out_ref[cls, WIN * B : ROWS, :] = tile[...].astype(jnp.bfloat16)
+    pltpu.make_async_copy(t_ref, t_ref, sems.at[2]).wait()
 
 
 def spread(where, t_now, t_cols, h_cols):
     return pl.pallas_call(
         spread_kernel,
         out_shape=[jax.ShapeDtypeStruct((GROUP, ROWS, B), jnp.bfloat16), jax.ShapeDtypeStruct((K,), jnp.int32)],
-        in_specs=[whole(pltpu.SMEM), whole(pltpu.HBM), whole(pltpu.HBM), whole()],
+        in_specs=[whole(pltpu.SMEM)] + [whole(pltpu.HBM)] * 3,
         out_specs=[whole(), whole(pltpu.SMEM)],
         scratch_shapes=[
             pltpu.SMEM((K, B), jnp.int32),
+            pltpu.VMEM(h_cols.shape, jnp.int32),
             pltpu.VMEM((EXTRA, B), jnp.float32),
-            pltpu.SemaphoreType.DMA,
-            pltpu.SemaphoreType.DMA,
+            pltpu.SemaphoreType.DMA((3,)),
         ],
         compiler_params=params(8),
         name="spread",
-    )(where, in_hbm(t_now), in_hbm(t_cols.T), h_cols)
-
-
-def pack_kernel(parts, where_ref, tab_ref, x_ref, *refs):
-    out_refs = refs[(len(refs) - len(parts)) // 2 :][: len(parts)]
+    )(where, *map(in_hbm, (t_now, t_cols.T, h_cols)))
+
+
+def pack_kernel(where_ref, tab_ref, x_ref, _, *refs):
+    *out_refs, sems = refs
     cls = where_ref[1]
-    for out_ref, part in zip(out_refs, parts):
-        for at in range(SIZES[part]):
-            entry = jnp.maximum(tab_ref[cls, STARTS[part] + at], 0)
+    for number, (out_ref, first, size) in enumerate(zip(out_refs, STARTS, SIZES)):
+        for at in range(size):
+            entry = jnp.maximum(tab_ref[cls, first + at], 0)
             start = pl.multiple_of(entry % WIN * B, B)
-            out_ref[at] = x_ref[entry // WIN, pl.ds(start, B), :]
-
-
-def pack(where, tab, x, parts, held):
-    return pl.pallas_call(
-        functools.partial(pack_kernel, parts),
-        out_shape=[jax.ShapeDtypeStruct((SIZES[part], B, B), jnp.bfloat16) for part in parts]
-        + [jax.ShapeDtypeStruct(h.shape, h.dtype) for h in held],
-        in_specs=[whole(pltpu.SMEM), whole(pltpu.SMEM), whole()] + [whole(pltpu.HBM)] * len(held),
-        out_specs=[whole()] * len(parts) + [whole(pltpu.HBM)] * len(held),
-        input_output_aliases={3 + i: len(parts) + i for i in range(len(held))},
-        compiler_params=params(8),
+            pltpu.make_async_copy(x_ref.at[entry // WIN, pl.ds(start, B)], out_ref.at[at], sems.at[number]).start()
+    for number, out_ref in enumerate(out_refs):
+        pltpu.make_async_copy(out_ref, out_ref, sems.at[number]).wait()
+
+
+def pack(where, tab, x, before):
+    return pl.pallas_call(
+        pack_kernel,
+        out_shape=[pltpu.HBM((size, B, B), jnp.bfloat16) for size in SIZES],
+        in_specs=[whole(pltpu.SMEM), whole(pltpu.SMEM), whole(pl.ANY), whole(pl.ANY)],
+        out_specs=[whole(pltpu.HBM)] * 4,
+        scratch_shapes=[pltpu.SemaphoreType.DMA((4,))],
+        compiler_params=params(4),
         name="pack",
-    )(where, tab, x, *map(in_hbm, held))
-
-
-def merge_kernel(first_ref, second_ref, out_ref, sems):
+    )(where, tab, x, before)
+
+
+def merge_kernel(first_ref, second_ref, out_ref, sem):
     half = first_ref.shape[0]
-    copies = [pltpu.make_async_copy(ref, out_ref.at[i * half : (i + 1) * half], sems.at[i]) for i, ref in enumerate((first_ref, second_ref))]
-    for copy in copies:
-        copy.start()
-    for copy in copies:
-        copy.wait()
+    load = pltpu.make_async_copy(first_ref, out_ref.at[0:half], sem)
+    load.start()
+    out_ref[half:] = second_ref[...]
+    load.wait()
 
 
 def merge(first, second):
     return pl.pallas_call(
         merge_kernel,
         out_shape=jax.ShapeDtypeStruct((2 * first.shape[0], *first.shape[1:]), first.dtype),
-        in_specs=[whole(pltpu.HBM)] * 2,
-        out_specs=whole(pltpu.HBM),
-        scratch_shapes=[pltpu.SemaphoreType.DMA((2,))],
-        compiler_params=params(4),
+        in_specs=[whole(pltpu.HBM), whole()],
+        out_specs=whole(),
+        scratch_shapes=[pltpu.SemaphoreType.DMA],
+        compiler_params=params(8),
         name="merge",
-    )(in_hbm(first), in_hbm(second))
+    )(in_hbm(first), second)
 
 
 def after_kernel(*_):
     pass
 
 
-def after(held, *first):
+def after(*held, hide=0):
     return pl.pallas_call(
         after_kernel,
-        out_shape=jax.ShapeDtypeStruct(held.shape, held.dtype),
-        in_specs=[whole(pltpu.HBM)] + [whole(pl.ANY)] * len(first),
-        out_specs=whole(pltpu.HBM),
-        input_output_aliases={0: 0},
+        out_shape=[jax.ShapeDtypeStruct(h.shape, h.dtype) for h in held],
+        in_specs=[whole(pl.ANY)] * len(held),
+        out_specs=[whole(pl.ANY)] * len(held),
+        input_output_aliases={i: i for i in range(len(held))},
         compiler_params=params(4),
+        cost_estimate=pl.CostEstimate(flops=hide, bytes_accessed=hide // 100, transcendentals=0),
         name="after",
-    )(in_hbm(held), *first)
+    )(*held)
 
 
 H_PARTS = (((0, 0),), ((0, 1),), ((-1, 0),), ((1, 1),), ((-1, 1), (2, 0)), ((1, 0), (2, 1)))
@@ -190,7 +195,10 @@
                 rows = pl.ds(pl.multiple_of(out_row * B, B), B)
                 for slot in range(K // N_LAYER):
                     at = h_at_ref[out_row, layer * (K // N_LAYER) + slot]
-                    pltpu.make_async_copy(h_ref.at[number * N_LAYER + r, slot], hd.at[at, rows], sem).start()
+                    if h_ref is h_refs[0] or h_ref is h_refs[1]:
+                        pltpu.make_async_copy(h_ref.at[r, slot], hd.at[at, rows], sem).start()
+                    else:
+                        hd[at, rows, :] = h_ref[number * N_LAYER + r, slot]
 
     @pl.loop(0, GROUP)
     def _(out_row):
@@ -209,7 +217,8 @@
             col = slot + (row > cls).astype(jnp.int32) + dist
             start = jnp.where(entry >= 0, (GROUP * (1 + dist) + row) * B, NEAR * B)
             xd[jnp.clip(col, 0, WIDE - 1), pl.ds(pl.multiple_of(start, B), B), :] = ref[i]
-    pltpu.make_async_copy(hd.at[0:K], hd.at[0:K], sem).wait()
+
+    pltpu.make_async_copy(hd.at[0 : K // N_LAYER], hd.at[0 : K // N_LAYER], sem).wait()
 
     @pl.loop(0, GROUP)
     def _(out_row):
@@ -232,17 +241,17 @@
             jax.ShapeDtypeStruct((GROUP, WIN, B, B), jnp.float32),
             jax.ShapeDtypeStruct((GROUP, GROUP * B, B), jnp.bfloat16),
         ],
-        in_specs=[whole(pltpu.SMEM)] * 3 + [whole()] * 5 + [whole(pltpu.HBM)] * len(h_parts),
+        in_specs=[whole(pltpu.SMEM)] * 3 + [whole()] * 5 + [whole(pltpu.HBM)] * 2 + [whole()] * (len(h_parts) - 2),
         out_specs=[whole()] * 2,
         scratch_shapes=[
             pltpu.VMEM((NEAR + GROUP, GROUP * B, B), jnp.bfloat16),
             pltpu.VMEM((WIDE, (NEAR + 1) * B, B), jnp.bfloat16),
             pltpu.SemaphoreType.DMA,
         ],
-        compiler_params=params(30),
+        compiler_params=params(22),
         cost_estimate=pl.CostEstimate(flops=2 * 1024 * 3072 * 512, bytes_accessed=20_000_000, transcendentals=0),
         name="near",
-    )(where, tab, h_at, x, rf, rn, lf, ln, *map(in_hbm, h_parts))
+    )(where, tab, h_at, x, rf, rn, lf, ln, *map(in_hbm, h_parts[:2]), *h_parts[2:])
 
 
 def far_kernel(where_ref, tab_ref, acc_ref, far_ref, r_ref, l_ref, out_ref, xd):
@@ -351,12 +360,13 @@
     h_one, h_other = along(h_vals), across(h_vals)
     spread_t, places = spread(where, t_now, t_cols, h_cols)
     x = exchange(spread_t)
-    held = (h_one, h_other, across(h_one), merge(h_other, h_one))
-    right_far, left_far, right_near, left_near, h_one, h_other, h_back, h_next = pack(where, tab, x, (0, 2, 1, 3), held)
+    h_back = across(h_one)
+    right_far, right_near, left_far, left_near = pack(where, tab, x, h_back)
     rf, lf = shift(right_far, 1), shift(left_far, -1)
     rn, ln = shift(right_near, 1), shift(left_near, -1)
-    h_next = after(along(h_next), rf, lf, rn, ln)
-    h_parts = [h_vals, h_other, h_one, h_back, h_next, across(h_next)]
+    h_next = along(merge(h_other, h_one))
+    (h_last,) = after(across(h_next), hide=10**12)
+    h_parts = [h_vals, h_other, h_one, h_back, h_next, h_last]
     h_at = x[:, WIN * B : WIN * B + N_LAYER, 0 : K // N_LAYER].astype(jnp.int32)
     h_at = (h_at - own_row // GROUP * GROUP + 2 * GROUP) % NB
     h_at = h_at.reshape(2, N_LAYER, N_LAYER, K // N_LAYER).transpose(0, 2, 1, 3).reshape(GROUP, K)
@@ -364,6 +374,7 @@
     is_near = jnp.logical_and(h_at >= GROUP, h_at < GROUP + NEAR)
     h_at = jnp.where(is_near, h_at - GROUP, NEAR + (h_at - out_rows) % GROUP)
     h_at = jnp.concatenate([h_at, absent(h_at, NEAR + GROUP)], axis=1)
+    rf, lf = after(rf, lf, hide=10**12)
     rff, lff = shift(rf, 1), shift(lf, -1)
     acc, far_h = near(where, tab, h_at, x, rf, rn, lf, ln, h_parts)
     sums = far(where, tab, acc, far_h, rff, lff)

time: 116 us -> 107 us (0.922)
  waiting for transfers between devices: 42.7 us -> 29.5 us
  starting transfers between devices: 41.2 us -> 47.8 us
  local copies, waits for them, and re-layouts: 6.37 us -> 0.27 us
  Pallas kernels: 23.1 us -> 27.3 us
    ppermute x6, waiting for transfers between devices: 26 us -> 6.57 us  [shift(): lax.ppermute(block, 'grid', [(i, (i + 2 * step) % count) for i in range(c...]
    unnamed x20 -> x4, local copies, waits for them, and re-layouts: 6.1 us -> 0.01 us
    ppermute x2, waiting for transfers between devices: 2.02 us -> 6.26 us  [along(): return lax.ppermute(block, axes, route)]
    all_to_all x1, starting transfers between devices: 4.72 us -> 8.58 us  [shards(): got = exchange(sums)]
    ppermute x6, starting transfers between devices: 17.5 us -> 13.8 us  [shift(): lax.ppermute(block, 'grid', [(i, (i + 2 * step) % count) for i in range(c...]
    ppermute x3, starting transfers between devices: 11 us -> 14.3 us  [across(): return lax.ppermute(block, 'grid', [(i, i ^ 1) for i in range(2 * chips)])]
    ppermute x2, starting transfers between devices: 3.47 us -> 6.58 us  [along(): return lax.ppermute(block, axes, route)]
    ppermute x3, waiting for transfers between devices: 0.01 us -> 1.64 us  [across(): return lax.ppermute(block, 'grid', [(i, i ^ 1) for i in range(2 * chips)])]
  transfers between devices with their start and end apart: 13 -> 13, of which waited for: 6 -> 8; matrix products, arithmetic and copies ran while one was open for 1% -> 1% of each run, Pallas kernels for 12% -> 17%
where the time goes in v3:
time: 107 us
  starting transfers between devices  47.8 us (45%)
  waiting for transfers between devices  29.5 us (28%)
  Pallas kernels  27.3 us (26%)
  between operations  1.52 us (1%)
    ppermute x3, starting transfers between devices, across(): return lax.ppermute(block, 'grid', [(i, i ^ 1) for i in range(2 * chips)])  14.3 us
    all_to_all x1, waiting for transfers between devices, shards(): got = exchange(sums)  14.3 us
    ppermute x6, starting transfers between devices, shift(): lax.ppermute(block, 'grid', [(i, (i + 2 * step) % count) for i in range(c...  13.8 us
    pallas_call x1, Pallas kernels, near(): pl.pallas_call(near_kernel, out_shape=[jax.ShapeDtypeStruct((GROUP, WIN,...  10.4 us
    all_to_all x1, starting transfers between devices, shards(): got = exchange(sums)  8.58 us
    ppermute x2, starting transfers between devices, along(): return lax.ppermute(block, axes, route)  6.58 us
    ppermute x6, waiting for transfers between devices, shift(): lax.ppermute(block, 'grid', [(i, (i + 2 * step) % count) for i in range(c...  6.57 us
    ppermute x2, waiting for transfers between devices, along(): return lax.ppermute(block, axes, route)  6.26 us
  transfers between devices with their start and end apart: 13, of which 8 were waited for; matrix products, arithmetic and copies ran while one was open for 1% of the time, Pallas kernels for 17%

profile of v3, /device:TPU:1, one launch (start us, length us, event | category | flops | bytes accessed | tf_op | source)
XLA Modules:
  0.0 107.0 jit_solution(15932940561379560776)
XLA Ops:
  0.6 3.4 %collective-permute-start = (bf16[4,7,128,128]{3,2,1,0:T(8,128)(2,1)}, bf16[4,7,128,128]{3,2,1,0:T(8,128)(2,1)}, u32[]{:S(2)}, u32[]{:S(2)}) collective-permute-start(bf16[4,7,128,128]{3,2,1,0:T(8,128)(2,1)} %refs_0_.1), channel_id=1, source_target_pairs={{0,1},{1,2},{2,3},{3,0},{4,7},{5,4},{6,5},{7,6},{8,9},{9,10},{10,1... | collective-permute-start | bytes 2752520 | tf_op jit(solution)/shard_map/ppermute | solution.py:351
  4.1 0.1 pad_add_fusion.1.where_ref
  4.1 3.8 %spread.1 = (bf16[8,528,128]{2,1,0:T(8,128)(2,1)}, s32[28]{0:T(128)S(1)}) custom-call(s32[2]{0:T(128)S(1)} %pad_add_fusion.1.where_ref, bf16[1,28,128,128]{3,2,1,0:T(8,128)(2,1)} %t_ref.1, s32[28,256]{1,0:T(8,128)} %bitcast.7, s32[4,7]{1,0:T(4,128)} %h_cols_ref.1), custom_call_target="tpu_custom_call" | custom-call | tf_op jit(solution)/shard_map/spread/pallas_call | solution.py:102
  8.0 4.5 %all-to-all-start = ((bf16[8,528,128]{2,1,0:T(8,128)(2,1)}), bf16[8,528,128]{2,1,0:T(8,128)(2,1)S(1)}, u32[]{:S(2)}, u32[]{:S(2)}) async-start(bf16[8,528,128]{2,1,0:T(8,128)(2,1)} %get-tuple-element.13), calls=%async_computation | async-start | bytes 2162688 | tf_op jit(solution)/shard_map/all_to_all | solution.py:362
  12.5 3.3 %collective-permute-done.second_ref.refs_2_ = bf16[4,7,128,128]{3,2,1,0:T(8,128)(2,1)} collective-permute-done((bf16[4,7,128,128]{3,2,1,0:T(8,128)(2,1)}, bf16[4,7,128,128]{3,2,1,0:T(8,128)(2,1)}, u32[]{:S(2)}, u32[]{:S(2)}) %collective-permute-start) | collective-permute-done | bytes 917536 | tf_op jit(solution)/shard_map/ppermute | solution.py:351
  15.8 2.4 %merge.1 = bf16[8,7,128,128]{3,2,1,0:T(8,128)(2,1)S(1)} custom-call(bf16[4,7,128,128]{3,2,1,0:T(8,128)(2,1)} %collective-permute-done.6.first_ref.refs_1_, bf16[4,7,128,128]{3,2,1,0:T(8,128)(2,1)} %collective-permute-done.second_ref.refs_2_), custom_call_target="tpu_custom_call" | custom-call | tf_op jit(solution)/shard_map/merge/pallas_call | solution.py:151
  18.1 3.2 %collective-permute-start.7 = (bf16[8,7,128,128]{3,2,1,0:T(8,128)(2,1)S(1)}, bf16[8,7,128,128]{3,2,1,0:T(8,128)(2,1)}, u32[]{:S(2)}, u32[]{:S(2)}) collective-permute-start(bf16[8,7,128,128]{3,2,1,0:T(8,128)(2,1)S(1)} %merge.1), channel_id=1, source_target_pairs={{0,1},{1,2},{2,3},{3,0},{4,7},{5,4},{6,5},{7,6},{8,9},{9,10},{10,1... | collective-permute-start | bytes 5505032 | tf_op jit(solution)/shard_map/ppermute | solution.py:351
  21.3 7.6 %collective-permute-start.1 = (bf16[4,7,128,128]{3,2,1,0:T(8,128)(2,1)}, bf16[4,7,128,128]{3,2,1,0:T(8,128)(2,1)}, u32[]{:S(2)}, u32[]{:S(2)}) collective-permute-start(bf16[4,7,128,128]{3,2,1,0:T(8,128)(2,1)} %collective-permute-done.second_ref.refs_2_), channel_id=1, source_target_pairs={{0,4},{4,0},{8,12},{12,8},{16,20},{20,16},{24,28},{28,24},{32,36},... | collective-permute-start | bytes 2752520 | tf_op jit(solution)/shard_map/ppermute | solution.py:354
  29.0 0.7 all-to-all-done.x_ref
  29.7 0.1 reshape.49
  29.8 1.6 %collective-permute-done.1._.refs_3_ = bf16[4,7,128,128]{3,2,1,0:T(8,128)(2,1)} collective-permute-done((bf16[4,7,128,128]{3,2,1,0:T(8,128)(2,1)}, bf16[4,7,128,128]{3,2,1,0:T(8,128)(2,1)}, u32[]{:S(2)}, u32[]{:S(2)}) %collective-permute-start.1) | collective-permute-done | bytes 917536 | tf_op jit(solution)/shard_map/ppermute | solution.py:354
  31.4 1.9 %pack.1 = (bf16[20,128,128]{2,1,0:T(8,128)(2,1)}, bf16[10,128,128]{2,1,0:T(8,128)(2,1)}, bf16[20,128,128]{2,1,0:T(8,128)(2,1)}, bf16[10,128,128]{2,1,0:T(8,128)(2,1)}) custom-call(s32[2]{0:T(128)S(1)} %pad_add_fusion.1.where_ref, s32[8,60]{1,0:T(8,128)S(1)} %copy-done.1, bf16[8,528,128]{2,1,0:T(8,128)(2,1)S(1)} %all-to-all-done.x_ref, ...), custom_call_target="tpu_custom_call" | custom-call | tf_op jit(solution)/shard_map/pack/pallas_call | solution.py:131
  33.3 0.1 collective-permute-start.2
  33.4 4.8 %collective-permute-start.3 = (bf16[20,128,128]{2,1,0:T(8,128)(2,1)}, bf16[20,128,128]{2,1,0:T(8,128)(2,1)}, u32[]{:S(2)}, u32[]{:S(2)}) collective-permute-start(bf16[20,128,128]{2,1,0:T(8,128)(2,1)} %get-tuple-element.15), channel_id=1, source_target_pairs={{0,248},{4,252},{8,0},{12,4},{16,8},{20,12},{24,16},{28,20},{32,24... | collective-permute-start | bytes 1966088 | tf_op jit(solution)/shard_map/ppermute | solution.py:347
  38.2 0.1 copy.15
  38.3 0.1 fusion
  38.4 0.2 convert_reduce_fusion
  38.6 0.1 select_reduce_fusion
  38.8 0.1 copy.16
  38.9 0.1 pad_add_fusion.h_at_ref
  38.9 4.8 %collective-permute-start.5 = (bf16[10,128,128]{2,1,0:T(8,128)(2,1)}, bf16[10,128,128]{2,1,0:T(8,128)(2,1)}, u32[]{:S(2)}, u32[]{:S(2)}) collective-permute-start(bf16[10,128,128]{2,1,0:T(8,128)(2,1)} %get-tuple-element.19), channel_id=1, source_target_pairs={{0,248},{4,252},{8,0},{12,4},{16,8},{20,12},{24,16},{28,20},{32,24... | collective-permute-start | bytes 983048 | tf_op jit(solution)/shard_map/ppermute | solution.py:347
  43.7 3.0 %collective-permute-done.7.refs_4_ = bf16[8,7,128,128]{3,2,1,0:T(8,128)(2,1)} collective-permute-done((bf16[8,7,128,128]{3,2,1,0:T(8,128)(2,1)S(1)}, bf16[8,7,128,128]{3,2,1,0:T(8,128)(2,1)}, u32[]{:S(2)}, u32[]{:S(2)}) %collective-permute-start.7) | collective-permute-done | bytes 1835040 | tf_op jit(solution)/shard_map/ppermute | solution.py:351
  46.7 6.7 %collective-permute-start.8 = (bf16[8,7,128,128]{3,2,1,0:T(8,128)(2,1)}, bf16[8,7,128,128]{3,2,1,0:T(8,128)(2,1)}, u32[]{:S(2)}, u32[]{:S(2)}) collective-permute-start(bf16[8,7,128,128]{3,2,1,0:T(8,128)(2,1)} %collective-permute-done.7.refs_4_), channel_id=1, source_target_pairs={{0,4},{4,0},{8,12},{12,8},{16,20},{20,16},{24,28},{28,24},{32,36},... | collective-permute-start | bytes 5505032 | tf_op jit(solution)/shard_map/ppermute | solution.py:354
  53.4 4.1 %collective-permute-start.10 = (bf16[20,128,128]{2,1,0:T(8,128)(2,1)}, bf16[20,128,128]{2,1,0:T(8,128)(2,1)}, u32[]{:S(2)}, u32[]{:S(2)}) collective-permute-start(bf16[20,128,128]{2,1,0:T(8,128)(2,1)} %get-tuple-element.18.lf_ref), channel_id=1, source_target_pairs={{0,248},{4,252},{8,0},{12,4},{16,8},{20,12},{24,16},{28,20},{32,24... | collective-permute-start | bytes 1966088 | tf_op jit(solution)/shard_map/ppermute | solution.py:347
  57.5 2.5 %collective-permute-done.4.rn_ref = bf16[10,128,128]{2,1,0:T(8,128)(2,1)} collective-permute-done((bf16[10,128,128]{2,1,0:T(8,128)(2,1)}, bf16[10,128,128]{2,1,0:T(8,128)(2,1)}, u32[]{:S(2)}, u32[]{:S(2)}) %collective-permute-start.4) | collective-permute-done | bytes 327712 | tf_op jit(solution)/shard_map/ppermute | solution.py:347
  60.0 10.4 %near.1 = (f32[8,4,128,128]{3,2,1,0:T(8,128)S(1)}, bf16[8,1024,128]{2,1,0:T(8,128)(2,1)S(1)}) custom-call(s32[2]{0:T(128)S(1)} %pad_add_fusion.1.where_ref, s32[8,60]{1,0:T(8,128)S(1)} %copy-done.1, s32[8,32]{1,0:T(8,128)S(1)} %pad_add_fusion.h_at_ref, bf16[8,528,128]{2,1,0:T(8,128)(2,1)S(1)} %all-to-all-done.x_ref, ...), custom_call_target="tpu_custom_call" | custom-call | flops 3221225472 | bytes 20000000 | tf_op jit(solution)/shard_map/near/pallas_call | solution.py:238
  70.4 2.4 %collective-permute-done.10.l_ref = bf16[20,128,128]{2,1,0:T(8,128)(2,1)} collective-permute-done((bf16[20,128,128]{2,1,0:T(8,128)(2,1)}, bf16[20,128,128]{2,1,0:T(8,128)(2,1)}, u32[]{:S(2)}, u32[]{:S(2)}) %collective-permute-start.10) | collective-permute-done | bytes 655392 | tf_op jit(solution)/shard_map/ppermute | solution.py:347
  72.8 1.7 %collective-permute-done.9.r_ref = bf16[20,128,128]{2,1,0:T(8,128)(2,1)} collective-permute-done((bf16[20,128,128]{2,1,0:T(8,128)(2,1)}, bf16[20,128,128]{2,1,0:T(8,128)(2,1)}, u32[]{:S(2)}, u32[]{:S(2)}) %collective-permute-start.9) | collective-permute-done | bytes 655392 | tf_op jit(solution)/shard_map/ppermute | solution.py:347
  74.5 5.6 %far.1 = bf16[8,4,128,128]{3,2,1,0:T(8,128)(2,1)} custom-call(s32[2]{0:T(128)S(1)} %pad_add_fusion.1.where_ref, s32[8,60]{1,0:T(8,128)S(1)} %copy-done.1, f32[8,4,128,128]{3,2,1,0:T(8,128)S(1)} %get-tuple-element.20.acc_ref, bf16[8,1024,128]{2,1,0:T(8,128)(2,1)S(1)} %get-tuple-element.21.far_ref, bf16[20,128,128]{2,1,0:T(8,128)(2,1)} %collective-permute-done.9.r_ref, ...), custom_call_target="tpu_custom_call" | custom-call | flops 1073741824 | bytes 8000000 | tf_op jit(solution)/shard_map/far/pallas_call | solution.py:281
  80.0 8.6 %all-to-all-start.1 = ((bf16[8,4,128,128]{3,2,1,0:T(8,128)(2,1)}), bf16[8,4,128,128]{3,2,1,0:T(8,128)(2,1)S(1)}, u32[]{:S(2)}, u32[]{:S(2)}) async-start(bf16[8,4,128,128]{3,2,1,0:T(8,128)(2,1)} %far.1), calls=%async_computation.1 | async-start | bytes 2097152 | tf_op jit(solution)/shard_map/all_to_all | solution.py:381
  89.3 14.3 %all-to-all-done.1.got_ref = bf16[8,4,128,128]{3,2,1,0:T(8,128)(2,1)S(1)} async-done(((bf16[8,4,128,128]{3,2,1,0:T(8,128)(2,1)}), bf16[8,4,128,128]{3,2,1,0:T(8,128)(2,1)S(1)}, u32[]{:S(2)}, u32[]{:S(2)}) %all-to-all-start.1) | async-done | bytes 1048608 | tf_op jit(solution)/shard_map/all_to_all | solution.py:381
  103.6 3.2 %update.1 = (bf16[1,28,128,128]{3,2,1,0:T(8,128)(2,1)}, f32[1,28,128,128]{3,2,1,0:T(8,128)}) custom-call(s32[28]{0:T(128)S(1)} %get-tuple-element.12.places_ref, f32[1]{0:T(128)S(6)} %copy.20.coef_ref, bf16[8,4,128,128]{3,2,1,0:T(8,128)(2,1)S(1)} %all-to-all-done.1.got_ref, f32[1,28,128,128]{3,2,1,0:T(8,128)S(1)} %copy-done, bf16[1,28,128,128]{3,2,1,0:T(8,128)(2,1)} %prev_hbm.1), custom_call_target="tpu_custom_call" | custom-call | tf_op jit(solution)/shard_map/update/pallas_call | solution.py:328
  (18 shorter events, 0.1 us)
Async XLA Ops:
  0.6 15.1 %collective-permute-start = (bf16[4,7,128,128]{3,2,1,0:T(8,128)(2,1)}, bf16[4,7,128,128]{3,2,1,0:T(8,128)(2,1)}, u32[]{:S(2)}, u32[]{:S(2)}) collective-permute-start(bf16[4,7,128,128]{3,2,1,0:T(8,128)(2,1)} %refs_0_.1), channel_id=1, source_target_pairs={{0,1},{1,2},{2,3},{3,0},{4,7},{5,4},{6,5},{7,6},{8,9},{9,10},{10,1... | collective-permute-start | bytes 2752520 | tf_op jit(solution)/shard_map/ppermute | solution.py:351
  4.0 11.8 %collective-permute-start.6 = (bf16[4,7,128,128]{3,2,1,0:T(8,128)(2,1)}, bf16[4,7,128,128]{3,2,1,0:T(8,128)(2,1)}, u32[]{:S(2)}, u32[]{:S(2)}) collective-permute-start(bf16[4,7,128,128]{3,2,1,0:T(8,128)(2,1)} %refs_0_.1), channel_id=1, source_target_pairs={{0,4},{4,0},{8,12},{12,8},{16,20},{20,16},{24,28},{28,24},{32,36},... | collective-permute-start | bytes 2752520 | tf_op jit(solution)/shard_map/ppermute | solution.py:354
  8.0 21.7 %all-to-all-start = ((bf16[8,528,128]{2,1,0:T(8,128)(2,1)}), bf16[8,528,128]{2,1,0:T(8,128)(2,1)S(1)}, u32[]{:S(2)}, u32[]{:S(2)}) async-start(bf16[8,528,128]{2,1,0:T(8,128)(2,1)} %get-tuple-element.13), calls=%async_computation | async-start | bytes 2162688 | tf_op jit(solution)/shard_map/all_to_all | solution.py:362
  12.5 18.9 %copy-start.1 = (s32[8,60]{1,0:T(8,128)S(1)}, s32[8,60]{1,0:T(8,128)}, u32[]{:S(2)}) copy-start(s32[8,60]{1,0:T(8,128)} %constant.77.clone.tab_ref) | copy-start | bytes 5764
  18.1 28.6 %collective-permute-start.7 = (bf16[8,7,128,128]{3,2,1,0:T(8,128)(2,1)S(1)}, bf16[8,7,128,128]{3,2,1,0:T(8,128)(2,1)}, u32[]{:S(2)}, u32[]{:S(2)}) collective-permute-start(bf16[8,7,128,128]{3,2,1,0:T(8,128)(2,1)S(1)} %merge.1), channel_id=1, source_target_pairs={{0,1},{1,2},{2,3},{3,0},{4,7},{5,4},{6,5},{7,6},{8,9},{9,10},{10,1... | collective-permute-start | bytes 5505032 | tf_op jit(solution)/shard_map/ppermute | solution.py:351
  21.3 10.1 %collective-permute-start.1 = (bf16[4,7,128,128]{3,2,1,0:T(8,128)(2,1)}, bf16[4,7,128,128]{3,2,1,0:T(8,128)(2,1)}, u32[]{:S(2)}, u32[]{:S(2)}) collective-permute-start(bf16[4,7,128,128]{3,2,1,0:T(8,128)(2,1)} %collective-permute-done.second_ref.refs_2_), channel_id=1, source_target_pairs={{0,4},{4,0},{8,12},{12,8},{16,20},{20,16},{24,28},{28,24},{32,36},... | collective-permute-start | bytes 2752520 | tf_op jit(solution)/shard_map/ppermute | solution.py:354
  33.3 20.1 %collective-permute-start.2 = (bf16[20,128,128]{2,1,0:T(8,128)(2,1)}, bf16[20,128,128]{2,1,0:T(8,128)(2,1)}, u32[]{:S(2)}, u32[]{:S(2)}) collective-permute-start(bf16[20,128,128]{2,1,0:T(8,128)(2,1)} %get-tuple-element.14), channel_id=1, source_target_pairs={{0,8},{4,12},{8,16},{12,20},{16,24},{20,28},{24,32},{28,36},{32,40... | collective-permute-start | bytes 1966088 | tf_op jit(solution)/shard_map/ppermute | solution.py:347
  33.4 20.0 %collective-permute-start.3 = (bf16[20,128,128]{2,1,0:T(8,128)(2,1)}, bf16[20,128,128]{2,1,0:T(8,128)(2,1)}, u32[]{:S(2)}, u32[]{:S(2)}) collective-permute-start(bf16[20,128,128]{2,1,0:T(8,128)(2,1)} %get-tuple-element.15), channel_id=1, source_target_pairs={{0,248},{4,252},{8,0},{12,4},{16,8},{20,12},{24,16},{28,20},{32,24... | collective-permute-start | bytes 1966088 | tf_op jit(solution)/shard_map/ppermute | solution.py:347
  38.9 21.0 %collective-permute-start.4 = (bf16[10,128,128]{2,1,0:T(8,128)(2,1)}, bf16[10,128,128]{2,1,0:T(8,128)(2,1)}, u32[]{:S(2)}, u32[]{:S(2)}) collective-permute-start(bf16[10,128,128]{2,1,0:T(8,128)(2,1)} %get-tuple-element.17), channel_id=1, source_target_pairs={{0,8},{4,12},{8,16},{12,20},{16,24},{20,28},{24,32},{28,36},{32,40... | collective-permute-start | bytes 983048 | tf_op jit(solution)/shard_map/ppermute | solution.py:347
  38.9 21.0 %collective-permute-start.5 = (bf16[10,128,128]{2,1,0:T(8,128)(2,1)}, bf16[10,128,128]{2,1,0:T(8,128)(2,1)}, u32[]{:S(2)}, u32[]{:S(2)}) collective-permute-start(bf16[10,128,128]{2,1,0:T(8,128)(2,1)} %get-tuple-element.19), channel_id=1, source_target_pairs={{0,248},{4,252},{8,0},{12,4},{16,8},{20,12},{24,16},{28,20},{32,24... | collective-permute-start | bytes 983048 | tf_op jit(solution)/shard_map/ppermute | solution.py:347
  46.7 10.8 %collective-permute-start.8 = (bf16[8,7,128,128]{3,2,1,0:T(8,128)(2,1)}, bf16[8,7,128,128]{3,2,1,0:T(8,128)(2,1)}, u32[]{:S(2)}, u32[]{:S(2)}) collective-permute-start(bf16[8,7,128,128]{3,2,1,0:T(8,128)(2,1)} %collective-permute-done.7.refs_4_), channel_id=1, source_target_pairs={{0,4},{4,0},{8,12},{12,8},{16,20},{20,16},{24,28},{28,24},{32,36},... | collective-permute-start | bytes 5505032 | tf_op jit(solution)/shard_map/ppermute | solution.py:354
  53.4 19.4 %collective-permute-start.10 = (bf16[20,128,128]{2,1,0:T(8,128)(2,1)}, bf16[20,128,128]{2,1,0:T(8,128)(2,1)}, u32[]{:S(2)}, u32[]{:S(2)}) collective-permute-start(bf16[20,128,128]{2,1,0:T(8,128)(2,1)} %get-tuple-element.18.lf_ref), channel_id=1, source_target_pairs={{0,248},{4,252},{8,0},{12,4},{16,8},{20,12},{24,16},{28,20},{32,24... | collective-permute-start | bytes 1966088 | tf_op jit(solution)/shard_map/ppermute | solution.py:347
  57.5 17.0 %collective-permute-start.9 = (bf16[20,128,128]{2,1,0:T(8,128)(2,1)}, bf16[20,128,128]{2,1,0:T(8,128)(2,1)}, u32[]{:S(2)}, u32[]{:S(2)}) collective-permute-start(bf16[20,128,128]{2,1,0:T(8,128)(2,1)} %get-tuple-element.16.rf_ref), channel_id=1, source_target_pairs={{0,8},{4,12},{8,16},{12,20},{16,24},{20,28},{24,32},{28,36},{32,40... | collective-permute-start | bytes 1966088 | tf_op jit(solution)/shard_map/ppermute | solution.py:347
  80.0 23.6 %copy-start = (f32[1,28,128,128]{3,2,1,0:T(8,128)S(1)}, f32[1,28,128,128]{3,2,1,0:T(8,128)}, u32[]{:S(2)}) copy-start(f32[1,28,128,128]{3,2,1,0:T(8,128)} %density_ref.1) | copy-start | bytes 5505028
  80.0 23.6 %all-to-all-start.1 = ((bf16[8,4,128,128]{3,2,1,0:T(8,128)(2,1)}), bf16[8,4,128,128]{3,2,1,0:T(8,128)(2,1)S(1)}, u32[]{:S(2)}, u32[]{:S(2)}) async-start(bf16[8,4,128,128]{3,2,1,0:T(8,128)(2,1)} %far.1), calls=%async_computation.1 | async-start | bytes 2097152 | tf_op jit(solution)/shard_map/all_to_all | solution.py:381
